TPU v7x, 256 devices: a whole 4x4x8 slice. The times are simulated.
256 devices in a mesh: col: 8 (over x_lo, y), tok: 32 (over z, x_hi, core).
Axes of the slice: x: 4 (x_hi: 2, x_lo: 2; x = x_hi * 2 + x_lo), y: 4, z: 8, core: 2. Of those that a mesh axis runs over, the one named last changes fastest.
Arguments:
- activations: bfloat16 [32768, 8192], P('tok', 'col'), may hold values from -6 to 6
Outputs:
- factor: float32 [8192, 8192], P(('col', 'tok'))
All inputs are finite; a program needn't handle non-finite values.
Results may differ from a plain program's by a relative error of at most 0.0003.
Values may be sent and summed in bfloat16 or wider, within the bound.
A program may use at most 128 MiB of HBM per device.

v0:
```python
import jax
import jax.numpy as jnp
from jax import lax
from jax.sharding import PartitionSpec as P

contract_first = (((0,), (0,)), ((), ()))


def passed_along(value, axis, by):
    size = lax.axis_size(axis)
    return lax.ppermute(value, axis, [(i, (i + by) % size) for i in range(size)])


def make_term(left_block, right_block):
    return lax.dot_general(
        left_block, right_block, contract_first, preferred_element_type=jnp.float32
    )


def shards(activations):
    block_width = activations.shape[1]
    token_ranks = lax.axis_size("tok")
    column_ranks = lax.axis_size("col")
    share_rows = block_width // token_ranks
    total_tokens = activations.shape[0] * token_ranks
    half_loop = column_ranks // 2
    fetched = [activations]
    for offset in range(1, half_loop + 1):
        fetched.append(passed_along(fetched[-1], "col", -1))
    tile_pairs = []
    for offset in range(half_loop + 1):
        tile_pairs.append((fetched[0], fetched[offset]))
    summed = [
        lax.psum_scatter(make_term(left_block, right_block), "tok", scatter_dimension=0, tiled=True)
        for left_block, right_block in tile_pairs
    ]
    pieces = [None] * column_ranks
    pieces[0] = summed[0]
    pieces[half_loop] = summed[half_loop]
    for offset in range(1, half_loop):
        reduced_tile = summed[offset]
        turned = lax.all_to_all(reduced_tile, "tok", split_axis=1, concat_axis=0, tiled=True).T
        own_piece, sent_piece = (reduced_tile, turned)
        pieces[offset] = own_piece
        pieces[column_ranks - offset] = passed_along(sent_piece, "col", offset)
    stacked = jnp.stack(pieces)
    ordered = jnp.roll(stacked, lax.axis_index("col"), axis=0)
    token_sums = jnp.transpose(ordered, (1, 0, 2)).reshape(share_rows, column_ranks * block_width)
    return token_sums / jnp.float32(total_tokens)


def solution(mesh):
    in_specs = (P("tok", "col"),)
    out_specs = P(("col", "tok"), None)
    return jax.shard_map(shards, mesh=mesh, in_specs=in_specs, out_specs=out_specs, check_vma=False)
```

profile of v0, /device:TPU:1, one launch (start us, length us, event | category | flops | bytes accessed | tf_op | source)
XLA Modules:
  0.0 721.1 jit_solution(852068615759597372)
XLA Ops:
  6.5 4.5 collective-permute-start
  11.0 44.6 %collective-permute-done = bf16[1024,1024]{1,0:T(8,128)(2,1)S(1)} collective-permute-done((bf16[1024,1024]{1,0:T(8,128)(2,1)}, bf16[1024,1024]{1,0:T(8,128)(2,1)S(1)}, u32[]{:S(2)}, u32[]{:S(2)}) %collective-permute-start) | collective-permute-done | bytes 2097184 | tf_op jit(solution)/shard_map/ppermute | solution.py:11
  57.0 6.0 fusion.1
  64.6 4.4 fusion
  69.0 4.3 collective-permute-start.1
  73.3 43.7 %collective-permute-done.1 = bf16[1024,1024]{1,0:T(8,128)(2,1)S(1)} collective-permute-done((bf16[1024,1024]{1,0:T(8,128)(2,1)}, bf16[1024,1024]{1,0:T(8,128)(2,1)S(1)}, u32[]{:S(2)}, u32[]{:S(2)}) %collective-permute-start.1) | collective-permute-done | bytes 2097184 | tf_op jit(solution)/shard_map/ppermute | solution.py:11
  118.3 4.4 fusion.2
  122.8 4.3 collective-permute-start.2
  127.1 48.5 %collective-permute-done.2 = bf16[1024,1024]{1,0:T(8,128)(2,1)S(1)} collective-permute-done((bf16[1024,1024]{1,0:T(8,128)(2,1)}, bf16[1024,1024]{1,0:T(8,128)(2,1)S(1)}, u32[]{:S(2)}, u32[]{:S(2)}) %collective-permute-start.2) | collective-permute-done | bytes 2097184 | tf_op jit(solution)/shard_map/ppermute | solution.py:11
  176.9 4.4 fusion.3
  181.3 4.5 collective-permute-start.3
  185.8 43.8 %collective-permute-done.3 = bf16[1024,1024]{1,0:T(8,128)(2,1)S(1)} collective-permute-done((bf16[1024,1024]{1,0:T(8,128)(2,1)}, bf16[1024,1024]{1,0:T(8,128)(2,1)S(1)}, u32[]{:S(2)}, u32[]{:S(2)}) %collective-permute-start.3) | collective-permute-done | bytes 2097184 | tf_op jit(solution)/shard_map/ppermute | solution.py:11
  229.6 4.3 fusion.4
  236.0 11.5 %all-to-all-start.2 = ((f32[32,1,1024]{2,1,0:T(1,128)}), f32[32,1,1024]{2,1,0:T(1,128)S(1)}, u32[]{:S(2)}, u32[]{:S(2)}) async-start(f32[32,1,1024]{2,1,0:T(1,128)} %reshape.16), calls=%async_computation.7 | async-start | bytes 262144 | tf_op jit(solution)/shard_map/all_to_all | solution.py:42
  247.6 74.2 %reduce-scatter.6.cloned.1.call-done = f32[32,1024]{1,0:T(8,128)} async-done(((f32[1024,1024]{1,0:T(8,128)}), f32[32,1024]{1,0:T(8,128)}) %reduce-scatter.6.cloned.1.call-update) | async-done | bytes 131088 | tf_op jit(solution)/shard_map/reduce_scatter | solution.py:34
  325.3 126.4 %reduce-scatter.10.cloned.1.call-done = f32[32,1024]{1,0:T(8,128)} async-done(((f32[1024,1024]{1,0:T(8,128)}), f32[32,1024]{1,0:T(8,128)}) %reduce-scatter.10.cloned.1.call-update) | async-done | bytes 131088 | tf_op jit(solution)/shard_map/reduce_scatter | solution.py:34
  453.7 10.8 %all-to-all-start.1 = ((f32[32,1,1024]{2,1,0:T(1,128)}), f32[32,1,1024]{2,1,0:T(1,128)S(1)}, u32[]{:S(2)}, u32[]{:S(2)}) async-start(f32[32,1,1024]{2,1,0:T(1,128)} %reshape.14), calls=%async_computation.6 | async-start | bytes 262144 | tf_op jit(solution)/shard_map/all_to_all | solution.py:42
  466.9 8.3 %all-to-all-done.1 = f32[32,1,1024]{2,1,0:T(1,128)S(1)} async-done(((f32[32,1,1024]{2,1,0:T(1,128)}), f32[32,1,1024]{2,1,0:T(1,128)S(1)}, u32[]{:S(2)}, u32[]{:S(2)}) %all-to-all-start.1) | async-done | bytes 131104 | tf_op jit(solution)/shard_map/all_to_all | solution.py:42
  476.4 105.2 %reduce-scatter.12.cloned.1.call-done = f32[32,1024]{1,0:T(8,128)} async-done(((f32[1024,1024]{1,0:T(8,128)}), f32[32,1024]{1,0:T(8,128)}) %reduce-scatter.12.cloned.1.call-update) | async-done | bytes 131088 | tf_op jit(solution)/shard_map/reduce_scatter | solution.py:34
  583.7 11.1 %all-to-all-start = ((f32[32,1,1024]{2,1,0:T(1,128)}), f32[32,1,1024]{2,1,0:T(1,128)S(1)}, u32[]{:S(2)}, u32[]{:S(2)}) async-start(f32[32,1,1024]{2,1,0:T(1,128)} %reshape.12), calls=%async_computation.5 | async-start | bytes 262144 | tf_op jit(solution)/shard_map/all_to_all | solution.py:42
  596.1 2.8 collective-permute-start.5
  598.9 6.7 all-to-all-done
  608.0 2.6 collective-permute-start.4
  610.6 101.5 %reduce-scatter.14.cloned.1.call-done = f32[32,1024]{1,0:T(8,128)} async-done(((f32[1024,1024]{1,0:T(8,128)}), f32[32,1024]{1,0:T(8,128)}) %reduce-scatter.14.cloned.1.call-update) | async-done | bytes 131088 | tf_op jit(solution)/shard_map/reduce_scatter | solution.py:34
  (74 shorter events, 24.8 us)
Async XLA Ops:
  6.5 227.4 %reduce-scatter.8.cloned.1.call-start = ((), (), s32[]{:S(2)}) async-start(), calls=%async_computation.9 | async-start | bytes 4325376 | tf_op jit(solution)/shard_map/reduce_scatter | solution.py:34
  6.5 49.1 %collective-permute-start = (bf16[1024,1024]{1,0:T(8,128)(2,1)}, bf16[1024,1024]{1,0:T(8,128)(2,1)S(1)}, u32[]{:S(2)}, u32[]{:S(2)}) collective-permute-start(bf16[1024,1024]{1,0:T(8,128)(2,1)} %param.1), channel_id=1, source_target_pairs={{0,224},{32,0},{64,32},{96,64},{128,96},{160,128},{192,160},{224,1... | collective-permute-start | bytes 6291464 | tf_op jit(solution)/shard_map/ppermute | solution.py:11
  55.6 1.4 copy-start.6
  63.0 1.6 copy-start.5
  63.0 258.8 %reduce-scatter.6.cloned.1.call-start = ((), (), s32[]{:S(2)}) async-start(), calls=%async_computation.8 | async-start | bytes 4325376 | tf_op jit(solution)/shard_map/reduce_scatter | solution.py:34
  68.9 382.7 %reduce-scatter.10.cloned.1.call-start = ((), (), s32[]{:S(2)}) async-start(), calls=%async_computation.10 | async-start | bytes 4325376 | tf_op jit(solution)/shard_map/reduce_scatter | solution.py:34
  69.0 48.0 %collective-permute-start.1 = (bf16[1024,1024]{1,0:T(8,128)(2,1)}, bf16[1024,1024]{1,0:T(8,128)(2,1)S(1)}, u32[]{:S(2)}, u32[]{:S(2)}) collective-permute-start(bf16[1024,1024]{1,0:T(8,128)(2,1)} %copy-done.6), channel_id=1, source_target_pairs={{0,224},{32,0},{64,32},{96,64},{128,96},{160,128},{192,160},{224,1... | collective-permute-start | bytes 6291464 | tf_op jit(solution)/shard_map/ppermute | solution.py:11
  117.0 1.3 copy-start.7
  122.7 458.9 %reduce-scatter.12.cloned.1.call-start = ((), (), s32[]{:S(2)}) async-start(), calls=%async_computation.11 | async-start | bytes 4325376 | tf_op jit(solution)/shard_map/reduce_scatter | solution.py:34
  122.8 52.8 %collective-permute-start.2 = (bf16[1024,1024]{1,0:T(8,128)(2,1)}, bf16[1024,1024]{1,0:T(8,128)(2,1)S(1)}, u32[]{:S(2)}, u32[]{:S(2)}) collective-permute-start(bf16[1024,1024]{1,0:T(8,128)(2,1)} %copy-done.7), channel_id=1, source_target_pairs={{0,224},{32,0},{64,32},{96,64},{128,96},{160,128},{192,160},{224,1... | collective-permute-start | bytes 6291464 | tf_op jit(solution)/shard_map/ppermute | solution.py:11
  175.6 1.3 copy-start.8
  181.3 530.8 %reduce-scatter.14.cloned.1.call-start = ((), (), s32[]{:S(2)}) async-start(), calls=%async_computation.12 | async-start | bytes 4325376 | tf_op jit(solution)/shard_map/reduce_scatter | solution.py:34
  181.3 48.2 %collective-permute-start.3 = (bf16[1024,1024]{1,0:T(8,128)(2,1)}, bf16[1024,1024]{1,0:T(8,128)(2,1)S(1)}, u32[]{:S(2)}, u32[]{:S(2)}) collective-permute-start(bf16[1024,1024]{1,0:T(8,128)(2,1)} %copy-done.8), channel_id=1, source_target_pairs={{0,224},{32,0},{64,32},{96,64},{128,96},{160,128},{192,160},{224,1... | collective-permute-start | bytes 6291464 | tf_op jit(solution)/shard_map/ppermute | solution.py:11
  236.0 87.6 %all-to-all-start.2 = ((f32[32,1,1024]{2,1,0:T(1,128)}), f32[32,1,1024]{2,1,0:T(1,128)S(1)}, u32[]{:S(2)}, u32[]{:S(2)}) async-start(f32[32,1,1024]{2,1,0:T(1,128)} %reshape.16), calls=%async_computation.7 | async-start | bytes 262144 | tf_op jit(solution)/shard_map/all_to_all | solution.py:42
  451.6 15.3 %copy-start.1 = (f32[32,1024]{1,0:T(8,128)S(1)}, f32[32,1024]{1,0:T(8,128)}, u32[]{:S(2)}) copy-start(f32[32,1024]{1,0:T(8,128)} %reduce-scatter.10.cloned.1.call-done) | copy-start | bytes 393220
  453.7 21.5 %all-to-all-start.1 = ((f32[32,1,1024]{2,1,0:T(1,128)}), f32[32,1,1024]{2,1,0:T(1,128)S(1)}, u32[]{:S(2)}, u32[]{:S(2)}) async-start(f32[32,1,1024]{2,1,0:T(1,128)} %reshape.14), calls=%async_computation.6 | async-start | bytes 262144 | tf_op jit(solution)/shard_map/all_to_all | solution.py:42
  465.7 247.4 %collective-permute-start.6 = (f32[32,1024]{1,0:T(8,128)}, f32[32,1024]{1,0:T(8,128)S(1)}, u32[]{:S(2)}, u32[]{:S(2)}) collective-permute-start(f32[32,1024]{1,0:T(8,128)} %bitcast.15), channel_id=1, source_target_pairs={{0,32},{32,64},{64,96},{96,128},{128,160},{160,192},{192,224},{224... | collective-permute-start | bytes 393224 | tf_op jit(solution)/shard_map/ppermute | solution.py:11
  581.6 17.3 %copy-start.2 = (f32[32,1024]{1,0:T(8,128)S(1)}, f32[32,1024]{1,0:T(8,128)}, u32[]{:S(2)}) copy-start(f32[32,1024]{1,0:T(8,128)} %reduce-scatter.12.cloned.1.call-done) | copy-start | bytes 393220
  583.7 21.9 %all-to-all-start = ((f32[32,1,1024]{2,1,0:T(1,128)}), f32[32,1,1024]{2,1,0:T(1,128)S(1)}, u32[]{:S(2)}, u32[]{:S(2)}) async-start(f32[32,1,1024]{2,1,0:T(1,128)} %reshape.12), calls=%async_computation.5 | async-start | bytes 262144 | tf_op jit(solution)/shard_map/all_to_all | solution.py:42
  596.1 117.0 %collective-permute-start.5 = (f32[32,1024]{1,0:T(8,128)}, f32[32,1024]{1,0:T(8,128)S(1)}, u32[]{:S(2)}, u32[]{:S(2)}) collective-permute-start(f32[32,1024]{1,0:T(8,128)} %bitcast.11), channel_id=1, source_target_pairs={{0,64},{32,96},{64,128},{96,160},{128,192},{160,224},{192,0},{224,... | collective-permute-start | bytes 393224 | tf_op jit(solution)/shard_map/ppermute | solution.py:11
  606.5 106.6 %copy-start.3 = (f32[32,1024]{1,0:T(8,128)S(1)}, f32[32,1024]{1,0:T(8,128)}, u32[]{:S(2)}) copy-start(f32[32,1024]{1,0:T(8,128)} %reduce-scatter.6.cloned.1.call-done) | copy-start | bytes 393220
  606.7 106.5 %copy-start = (f32[32,1024]{1,0:T(8,128)S(1)}, f32[32,1024]{1,0:T(8,128)}, u32[]{:S(2)}) copy-start(f32[32,1024]{1,0:T(8,128)} %reduce-scatter.8.cloned.1.call-done) | copy-start | bytes 393220
  608.0 105.1 %collective-permute-start.4 = (f32[32,1024]{1,0:T(8,128)}, f32[32,1024]{1,0:T(8,128)S(1)}, u32[]{:S(2)}, u32[]{:S(2)}) collective-permute-start(f32[32,1024]{1,0:T(8,128)} %bitcast.68), channel_id=1, source_target_pairs={{0,96},{32,128},{64,160},{96,192},{128,224},{160,0},{192,32},{224,... | collective-permute-start | bytes 393224 | tf_op jit(solution)/shard_map/ppermute | solution.py:11
  712.1 1.2 copy-start.4
Sparse Core Ops, SparseCore 0:
  63.1 128.7 reduce-scatter.7
  196.8 124.9 reduce-scatter.5
  326.0 125.5 reduce-scatter.9
  456.3 125.2 reduce-scatter.11
  585.7 126.3 reduce-scatter.13
where the time goes:
time: 725 us; the launch traced here: 721 us
  waiting for transfers between devices  603 us (83%)
  starting transfers between devices  57.7 us (8%)
  matrix products  23.4 us (3%)
  local copies, waits for them, and re-layouts  20.5 us (3%)
  between operations  13.5 us (2%)
    reduce_scatter x5, waiting for transfers between devices, shards(): lax.psum_scatter(make_term(left_block, right_block), 'tok', scatter_dimen...  407 us
    ppermute x7, waiting for transfers between devices, passed_along(): lax.ppermute(value, axis, [(i, (i + by) % size) for i in range(size)])  181 us
    all_to_all x3, starting transfers between devices, shards(): lax.all_to_all(reduced_tile, 'tok', split_axis=1, concat_axis=0, tiled=True)  33.4 us
    ppermute x7, starting transfers between devices, passed_along(): lax.ppermute(value, axis, [(i, (i + by) % size) for i in range(size)])  24.1 us
    dot_general x5, matrix products, make_term(): lax.dot_general(left_block, right_block, contract_first, preferred_elemen...  23.4 us
    all_to_all x3, waiting for transfers between devices, shards(): lax.all_to_all(reduced_tile, 'tok', split_axis=1, concat_axis=0, tiled=True)  15 us
  transfers between devices with their start and end apart: 15, of which 10 were waited for; matrix products, arithmetic and copies ran while one was open for 4% of the time, Pallas kernels for 0%

commit v1 on v0

v1 whole, which is shorter than its diff:
```python
import jax
import jax.numpy as jnp
from jax import lax
from jax.experimental import pallas as pl
from jax.experimental.pallas import tpu as pltpu
from jax.sharding import PartitionSpec as P

MESH = pl.DeviceIdType.MESH
F32, BF16 = jnp.float32, jnp.bfloat16
BLOCK = 1024
HALF = BLOCK // 2
ROWS = 32
W = 192
LAST = (((1,), (1,)), ((), ()))
C_NEXT_OWN, C_SELF_OWN, C_NEXT_OTHER, C_OPPOSITE, C_SELF_OTHER = range(5)
CELL_REL = (1, 0, 1, 2, 0)
MIRRORED = (C_NEXT_OWN, C_NEXT_OTHER, C_OPPOSITE)


def kernel(scale, a_ref, out_ref, G, Q, RL, T, CR, ZR, R, O1, O2, MB, MT, MO,
           xs, xr, ys, yr, cs, cr, zs, zr, ds, dr, ms, mr, ts, tr):
    col, tok = lax.axis_index("col"), lax.axis_index("tok")
    lo, y = col // 4, col % 4
    z, hi, c = tok // 4, (tok // 2) % 2, tok % 2
    x = 2 * hi + lo
    s = y // 2

    def at(x_, y_, z_, c_):
        return ((x_ % 2) * 4 + y_, z_ * 4 + (x_ // 2) * 2 + c_)

    x_next, x_prev = (x + 1) % 4, (x + 3) % 4
    y_next, y_prev, y_far = (y + 1) % 4, (y + 3) % 4, (y + 2) % 4
    x_dev = (at(x_next, y, z, c), at(x_prev, y, z, c))
    y_up, y_down = at(x, y_next, z, c), at(x, y_prev, z, c)
    sibling = at(x, y, z, 1 - c)
    z_dev = (at(x, y, (z + 1) % 8, c), at(x, y, (z + 7) % 8, c))
    pending = []

    def send(src, dst, s_sem, r_sem, dev):
        cp = pltpu.make_async_remote_copy(src_ref=src, dst_ref=dst, send_sem=s_sem, recv_sem=r_sem,
                                          device_id=dev, device_id_type=MESH)
        cp.start()
        pending.append(cp)
        return cp

    def arrived(dst, s_sem, r_sem):
        pltpu.make_async_remote_copy(src_ref=dst, dst_ref=dst, send_sem=s_sem, recv_sem=r_sem,
                                     device_id=sibling, device_id_type=MESH).wait_recv()

    partners = [at(2 * (hi ^ dh) + (lo ^ dl), y, z, c ^ dc)
                for dh in range(2) for dl in range(2) for dc in range(2) if dh + dl + dc]
    partners += [at(x, y, (z + dz) % 8, c) for dz in range(1, 8)]
    partners += [at(x, (y + dy) % 4, z, c) for dy in range(1, 4)]
    barrier = pltpu.get_barrier_semaphore()
    for dev in partners:
        pl.semaphore_signal(barrier, inc=1, device_id=dev, device_id_type=MESH)
    pl.semaphore_wait(barrier, len(partners))

    def reorder(h, part):
        p = lax.broadcasted_iota(jnp.int32, (BLOCK, HALF), 1)
        f = lax.broadcasted_iota(jnp.int32, (BLOCK, HALF), 0)
        feature = ((p // 32) % 8) * 128 + h * 64 + (p // 256) * 32 + p % 32
        pick = (f == feature).astype(F32).astype(BF16)
        rows = pl.ds(part * HALF, HALF)
        G[x, h, rows, :] = jnp.dot(a_ref[rows, :], pick, preferred_element_type=F32).astype(BF16)

    def turn(x_from, slot):
        r = lax.broadcasted_iota(jnp.int32, (HALF, HALF), 0)
        f = lax.broadcasted_iota(jnp.int32, (HALF, HALF), 1)
        one = (r == f).astype(F32).astype(BF16)
        Q[0, slot] = lax.dot_general(one, G[x_from, hi], LAST, preferred_element_type=F32).astype(BF16)

    def x_unit(x_, h, part):
        return G.at[x_, h, pl.ds(part * HALF, HALF), :]

    def x_send(d, step, x_, h, part):
        return send(x_unit(x_, h, part), x_unit(x_, h, part), xs.at[d, step], xr.at[d, step], x_dev[d])

    x_from = (x_prev, x_next)

    def x_arrived(d, step, h, part):
        arrived(x_unit(x_from[d], h, part), xs.at[d, step], xr.at[d, step])

    def h_of(x_):
        return x_ // 2

    def y_sends(k, slot):
        low, high = pl.ds(0, W), pl.ds(W, HALF - W)
        send(Q.at[0, slot, low], Q.at[1, slot, low], ys.at[k, 0], yr.at[k, 0], y_down)
        send(Q.at[0, slot, high], RL.at[k], ys.at[k, 2], yr.at[k, 2], y_up)
        send(Q.at[0, slot, high], Q.at[1, slot, high], ys.at[k, 1], yr.at[k, 1], y_down)

    def y_forward(k, slot):
        low, high = pl.ds(0, W), pl.ds(W, HALF - W)
        arrived(Q.at[1, slot, low], ys.at[k, 0], yr.at[k, 0])
        send(Q.at[1, slot, low], Q.at[2, slot, low], ys.at[k, 3], yr.at[k, 3], y_down)
        arrived(RL.at[k], ys.at[k, 2], yr.at[k, 2])
        send(RL.at[k], Q.at[2, slot, high], ys.at[k, 4], yr.at[k, 4], y_up)

    cell_lo = (lo, lo, 1 - lo, (lo + s) % 2, 1 - lo)

    def compute(cell):
        rel, l = CELL_REL[cell], cell_lo[cell]

        @pl.loop(0, 4)
        def _(n):
            h, cols = n // 2, pl.ds(pl.multiple_of((n % 2) * 256, 256), 256)
            acc = jnp.dot(Q[rel, 0], G[l, h, :, cols], preferred_element_type=F32)
            acc += jnp.dot(Q[rel, 1], G[2 + l, h, :, cols], preferred_element_type=F32)
            T[cell, :, :, :, pl.ds(pl.multiple_of(n * 256, 256), 256)] = acc.reshape(2, 8, ROWS, 256)

        send(T.at[cell, 1 - c], CR.at[cell], cs.at[cell], cr.at[cell], sibling)

    def core_arrived(cell):
        arrived(CR.at[cell], cs.at[cell], cr.at[cell])

    sides = (pl.ds(0, HALF), pl.ds(HALF, HALF))

    def z_landed(cell, d, step):
        part = ZR.at[cell, d, 0, :, sides[d]] if step == 0 else ZR.at[cell, d, step]
        arrived(part, zs.at[cell, d, step], zr.at[cell, d, step])

    def z_step(cell, step):
        for d in range(2):
            to = (z + 4 - step) % 8 if d == 0 else (z + 4 + step) % 8
            if step > 0:
                z_landed(cell, d, step - 1)
            if step == 0:
                cols = sides[d]
                T[cell, c, to, :, cols] = T[cell, c, to, :, cols] + CR[cell, to, :, cols]
                send(T.at[cell, c, to, :, cols], ZR.at[cell, d, 0, :, cols], zs.at[cell, d, 0], zr.at[cell, d, 0], z_dev[d])
                continue
            if step == 1:
                cols, rest = sides[d], sides[1 - d]
                T[cell, c, to, :, cols] = T[cell, c, to, :, cols] + CR[cell, to, :, cols] + ZR[cell, d, 0, :, cols]
                T[cell, c, to, :, rest] = T[cell, c, to, :, rest] + CR[cell, to, :, rest]
            else:
                T[cell, c, to] = T[cell, c, to] + CR[cell, to] + ZR[cell, d, step - 1]
            send(T.at[cell, c, to], ZR.at[cell, d, step], zs.at[cell, d, step], zr.at[cell, d, step], z_dev[d])

    def total(cell):
        z_landed(cell, 0, 3)
        z_landed(cell, 1, 3)
        return (T[cell, c, z] + CR[cell, z] + ZR[cell, 0, 3] + ZR[cell, 1, 3]) * scale

    def natural(v):
        return jnp.concatenate([v[:, h * HALF + k * 256 + b * 32:h * HALF + k * 256 + b * 32 + 32]
                                for b in range(8) for h in range(2) for k in range(2)], axis=1)

    def out_cols(l, y_):
        return pl.ds(pl.multiple_of((l * 4 + y_) * BLOCK, BLOCK), BLOCK)

    def group(h, k):
        return pl.ds(pl.multiple_of(h * HALF + k * 256, 256), 256)

    def mirror_slot(m, h, k, l):
        return (8 if m == 2 else l * 4) + h * 2 + k

    def spread(m):
        cell = MIRRORED[m]
        R[m] = total(cell)
        if m == 2:
            send(R.at[m], O2, ds.at[m], dr.at[m], at(x, y_far, z, c))
        else:
            send(R.at[m], O1.at[cell_lo[cell]], ds.at[m], dr.at[m], y_up)
        mine = mirror_slot(m, hi, c, lo)
        for dh in range(2):
            for dc in range(2):
                h, k = (hi + dh) % 2, (c + dc) % 2
                src = R.at[m, :, group(h, k)]
                dev = at(2 * h + cell_lo[cell], y, z, k)
                if dh + dc or m == 1:
                    send(src, MB.at[mine], ms.at[m, dh, dc], mr.at[m, dh, dc], dev)
                elif m == 0:
                    MB[mine] = R[m, :, group(h, k)]
                else:
                    @pl.when(s == 0)
                    def _():
                        MB[mine] = R[m, :, group(h, k)]

                    @pl.when(s == 1)
                    def _():
                        pltpu.make_async_remote_copy(
                            src_ref=src, dst_ref=MB.at[mine], send_sem=ms.at[m, dh, dc], recv_sem=mr.at[m, dh, dc],
                            device_id=dev, device_id_type=MESH).start()

    def spread_arrived():
        for m in range(3):
            l = (lo, 1 - lo, (lo + s) % 2)[m]
            for dh in range(2):
                for dc in range(2):
                    slot = mirror_slot(m, (hi + dh) % 2, (c + dc) % 2, l)
                    if dh + dc or m == 1:
                        arrived(MB.at[slot], ms.at[m, dh, dc], mr.at[m, dh, dc])
                    elif m == 2:
                        @pl.when(s == 1)
                        def _():
                            cp = pltpu.make_async_remote_copy(
                                src_ref=MB.at[slot], dst_ref=MB.at[slot], send_sem=ms.at[m, dh, dc],
                                recv_sem=mr.at[m, dh, dc], device_id=sibling, device_id_type=MESH)
                            cp.wait_recv()
                            cp.wait_send()

    for part in range(2):
        reorder(1 - hi, part)
        x_send(part, 0, x, 1 - hi, part)
    for part in range(2):
        reorder(hi, part)
    turn(x, hi)
    y_sends(0, hi)
    for d in range(2):
        x_arrived(d, 0, 1 - h_of(x_from[d]), d)
        x_send(d, 1, x_from[d], 1 - h_of(x_from[d]), d)
    y_forward(0, hi)
    x_opposite = (x + 2) % 4
    for d in range(2):
        arrived(x_unit(x_opposite, hi, d), xs.at[d, 1], xr.at[d, 1])
        x_send(d, 2, x, hi, d)
    turn(x_opposite, 1 - hi)
    y_sends(1, 1 - hi)
    for d in range(2):
        x_arrived(d, 2, h_of(x_from[d]), d)
        x_send(d, 3, x_from[d], h_of(x_from[d]), d)
    y_forward(1, 1 - hi)
    for d in range(2):
        arrived(x_unit(x_opposite, 1 - hi, d), xs.at[d, 3], xr.at[d, 3])
        x_send(d, 4, x, 1 - hi, 1 - d)
        x_send(d, 5, x, hi, 1 - d)

    compute(C_SELF_OWN)
    core_arrived(C_SELF_OWN)
    z_step(C_SELF_OWN, 0)
    high = pl.ds(W, HALF - W)
    for k, slot in ((0, hi), (1, 1 - hi)):
        arrived(Q.at[1, slot, high], ys.at[k, 1], yr.at[k, 1])
    compute(C_NEXT_OWN)
    z_step(C_SELF_OWN, 1)
    core_arrived(C_NEXT_OWN)
    z_step(C_NEXT_OWN, 0)
    z_step(C_SELF_OWN, 2)
    z_step(C_NEXT_OWN, 1)
    z_step(C_SELF_OWN, 3)
    z_step(C_NEXT_OWN, 2)
    for d in range(2):
        x_arrived(d, 4, 1 - h_of(x_from[d]), 1 - d)
        x_arrived(d, 5, h_of(x_from[d]), 1 - d)
    compute(C_NEXT_OTHER)
    z_step(C_NEXT_OWN, 3)
    for k, slot in ((0, hi), (1, 1 - hi)):
        arrived(Q.at[2, slot, pl.ds(0, W)], ys.at[k, 3], yr.at[k, 3])
        arrived(Q.at[2, slot, high], ys.at[k, 4], yr.at[k, 4])
    core_arrived(C_NEXT_OTHER)
    z_step(C_NEXT_OTHER, 0)
    compute(C_OPPOSITE)
    spread(0)
    z_step(C_NEXT_OTHER, 1)
    core_arrived(C_OPPOSITE)
    z_step(C_OPPOSITE, 0)
    compute(C_SELF_OTHER)
    z_step(C_NEXT_OTHER, 2)
    z_step(C_OPPOSITE, 1)
    core_arrived(C_SELF_OTHER)
    z_step(C_SELF_OTHER, 0)
    z_step(C_NEXT_OTHER, 3)
    z_step(C_OPPOSITE, 2)
    z_step(C_SELF_OTHER, 1)
    spread(1)
    z_step(C_OPPOSITE, 3)
    z_step(C_SELF_OTHER, 2)
    spread(2)
    z_step(C_SELF_OTHER, 3)
    spread_arrived()
    turned = jnp.transpose(MB[...].reshape(12 * ROWS, 256)).reshape(8, ROWS, 12 * ROWS)
    MT[...] = turned
    MO[z] = MT[z]
    for dz in range(1, 8):
        to = (z + dz) % 8
        send(MT.at[to], MO.at[z], ts.at[dz], tr.at[dz], at(x, y, to, c))
    out_ref[:, out_cols(lo, y)] = natural(total(C_SELF_OWN))
    out_ref[:, out_cols(1 - lo, y)] = natural(total(C_SELF_OTHER))
    for m, l in ((0, lo), (1, 1 - lo)):
        arrived(O1.at[l], ds.at[m], dr.at[m])
        out_ref[:, out_cols(l, y_prev)] = natural(O1[l])
    arrived(O2, ds.at[2], dr.at[2])
    out_ref[:, out_cols((lo + 1 - s) % 2, y_far)] = natural(O2[...])
    for dz in range(1, 8):
        arrived(MO.at[(z + 8 - dz) % 8], ts.at[dz], tr.at[dz])
    for l in range(2):
        out_ref[:, out_cols(l, y_next)] = jnp.concatenate([MO[b, :, l * 128:l * 128 + 128] for b in range(8)], axis=1)
    out_ref[:, out_cols((lo + s) % 2, y_far)] = jnp.concatenate([MO[b, :, 256:384] for b in range(8)], axis=1)
    for cp in pending:
        cp.wait_send()


def solution(mesh):
    token_ranks = mesh.shape["tok"]

    def shards(activations):
        scale = 1.0 / (activations.shape[0] * token_ranks)
        dma = pltpu.SemaphoreType.DMA
        return pl.pallas_call(
            lambda *refs: kernel(scale, *refs),
            out_shape=jax.ShapeDtypeStruct((ROWS, 8 * BLOCK), F32),
            in_specs=[pl.BlockSpec(memory_space=pltpu.VMEM)],
            out_specs=pl.BlockSpec(memory_space=pltpu.VMEM),
            scratch_shapes=[
                pltpu.VMEM((4, 2, BLOCK, HALF), BF16),
                pltpu.VMEM((3, 2, HALF, BLOCK), BF16),
                pltpu.VMEM((2, HALF - W, BLOCK), BF16),
                pltpu.VMEM((5, 2, 8, ROWS, BLOCK), F32),
                pltpu.VMEM((5, 8, ROWS, BLOCK), F32),
                pltpu.VMEM((5, 2, 4, ROWS, BLOCK), F32),
                pltpu.VMEM((3, ROWS, BLOCK), F32),
                pltpu.VMEM((2, ROWS, BLOCK), F32),
                pltpu.VMEM((ROWS, BLOCK), F32),
                pltpu.VMEM((12, ROWS, 256), F32),
                pltpu.VMEM((8, ROWS, 12 * ROWS), F32),
                pltpu.VMEM((8, ROWS, 12 * ROWS), F32),
                dma((2, 6)), dma((2, 6)),
                dma((2, 5)), dma((2, 5)),
                dma((5,)), dma((5,)),
                dma((5, 2, 4)), dma((5, 2, 4)),
                dma((3,)), dma((3,)),
                dma((3, 2, 2)), dma((3, 2, 2)),
                dma((8,)), dma((8,)),
            ],
            compiler_params=pltpu.CompilerParams(
                collective_id=0, has_side_effects=True, vmem_limit_bytes=56 * 1024 * 1024),
            cost_estimate=pl.CostEstimate(flops=14 * 10**9, bytes_accessed=3 * 2**20, transcendentals=0),
            name="gram",
        )(activations)

    return jax.shard_map(shards, mesh=mesh, in_specs=(P("tok", "col"),), out_specs=P(("col", "tok"), None), check_vma=False)
```

time: 725 us -> 142 us (0.20)
  waiting for transfers between devices: 603 us -> 0 us
  Pallas kernels: 0 us -> 140 us
  starting transfers between devices: 57.7 us -> 0 us
  matrix products: 23.4 us -> 0 us
  local copies, waits for them, and re-layouts: 20.5 us -> 2.26 us
  between operations: 13.5 us -> 0.01 us
    reduce_scatter x5 -> x0, waiting for transfers between devices: 407 us -> none  [shards(): lax.psum_scatter(make_term(left_block, right_block), 'tok', scatter_dimen...]
    ppermute x7 -> x0, waiting for transfers between devices: 181 us -> none  [passed_along(): lax.ppermute(value, axis, [(i, (i + by) % size) for i in range(size)])]
    pallas_call x0 -> x1, Pallas kernels: none -> 140 us  [shards(): pl.pallas_call(lambda *refs: kernel(scale, *refs), out_shape=jax.ShapeDty...]
    all_to_all x3 -> x0, starting transfers between devices: 33.4 us -> none  [shards(): lax.all_to_all(reduced_tile, 'tok', split_axis=1, concat_axis=0, tiled=True)]
    ppermute x7 -> x0, starting transfers between devices: 24.1 us -> none  [passed_along(): lax.ppermute(value, axis, [(i, (i + by) % size) for i in range(size)])]
    dot_general x5 -> x0, matrix products: 23.4 us -> none  [make_term(): lax.dot_general(left_block, right_block, contract_first, preferred_elemen...]
    all_to_all x3 -> x0, waiting for transfers between devices: 15 us -> none  [shards(): lax.all_to_all(reduced_tile, 'tok', split_axis=1, concat_axis=0, tiled=True)]
    unnamed x39 -> x1, local copies, waits for them, and re-layouts: 11.7 us -> 2.26 us
  transfers between devices with their start and end apart: 15 -> 0, of which waited for: 10 -> 0; matrix products, arithmetic and copies ran while one was open for 4% -> 0% of each run, Pallas kernels for 0% -> 0%
where the time goes in v1:
time: 142 us
  Pallas kernels  140 us (99%)
  local copies, waits for them, and re-layouts  2.26 us (2%)
    pallas_call x1, Pallas kernels, shards(): pl.pallas_call(lambda *refs: kernel(scale, *refs), out_shape=jax.ShapeDty...  140 us

profile of v1, /device:TPU:1, one launch (start us, length us, event | category | flops | bytes accessed | tf_op | source)
XLA Modules:
  0.0 142.0 jit_solution(12388333906909696285)
XLA Ops:
  0.0 139.8 %gram.1 = f32[32,8192]{1,0:T(8,128)} custom-call(bf16[1024,1024]{1,0:T(8,128)(2,1)} %refs_0_.1), custom_call_target="tpu_custom_call" | custom-call | flops 14000000000 | bytes 3145728 | tf_op jit(solution)/shard_map/gram/pallas_call | solution.py:301
  139.8 2.3 %copy.3 = f32[32,8192]{1,0:T(8,128)} copy(f32[32,8192]{1,0:T(8,128)} %gram.1) | data formatting | bytes 2097152

commit v2 on v1

v2 whole, which is shorter than its diff:
```python
import jax
import jax.numpy as jnp
from jax import lax
from jax.experimental import pallas as pl
from jax.experimental.pallas import tpu as pltpu
from jax.sharding import PartitionSpec as P

MESH = pl.DeviceIdType.MESH
F32, BF16 = jnp.float32, jnp.bfloat16
BLOCK = 1024
HALF = BLOCK // 2
ROWS = 32
W = 160
LAST = (((1,), (1,)), ((), ()))
CELLS = 12
OWN = (0, 1, 2, 3)
CELL_REL = (0, 0, None, None, 0, 1, 1, 1, 1, 2, 2, 0)
TO_NEXT = (5, 6, 7, 8)
TO_FAR = (9, 10)


def kernel(scale, a_ref, out_ref, G, Q, QP, RL, T, CR, ZR, R, PR, O1, O2, MB, MT, MO, OUT,
           xs, xr, ys, yr, cs, cr, zs, zr, ds, dr, ms, mr, ts, tr, os):
    col, tok = lax.axis_index("col"), lax.axis_index("tok")
    lo, y = col // 4, col % 4
    z, hi, c = tok // 4, (tok // 2) % 2, tok % 2
    x = 2 * hi + lo
    s = y // 2

    def at(x_, y_, z_, c_):
        return ((x_ % 2) * 4 + y_, z_ * 4 + (x_ // 2) * 2 + c_)

    x_next, x_prev = (x + 1) % 4, (x + 3) % 4
    y_next, y_prev, y_far = (y + 1) % 4, (y + 3) % 4, (y + 2) % 4
    x_dev = (at(x_next, y, z, c), at(x_prev, y, z, c))
    y_up, y_down = at(x, y_next, z, c), at(x, y_prev, z, c)
    sibling = at(x, y, z, 1 - c)
    z_dev = (at(x, y, (z + 1) % 8, c), at(x, y, (z + 7) % 8, c))
    pending = []

    def send(src, dst, s_sem, r_sem, dev):
        cp = pltpu.make_async_remote_copy(src_ref=src, dst_ref=dst, send_sem=s_sem, recv_sem=r_sem,
                                          device_id=dev, device_id_type=MESH)
        cp.start()
        pending.append(cp)
        return cp

    def arrived(dst, s_sem, r_sem):
        pltpu.make_async_remote_copy(src_ref=dst, dst_ref=dst, send_sem=s_sem, recv_sem=r_sem,
                                     device_id=sibling, device_id_type=MESH).wait_recv()

    partners = [at(2 * (hi ^ dh) + (lo ^ dl), y, z, c ^ dc)
                for dh in range(2) for dl in range(2) for dc in range(2) if dh + dl + dc]
    partners += [at(x, y, (z + dz) % 8, c) for dz in range(1, 8)]
    partners += [at(x, (y + dy) % 4, z, c) for dy in range(1, 4)]
    barrier = pltpu.get_barrier_semaphore()
    for dev in partners:
        pl.semaphore_signal(barrier, inc=1, device_id=dev, device_id_type=MESH)

    def reorder(h, part):
        p = lax.broadcasted_iota(jnp.int32, (BLOCK, HALF), 1)
        f = lax.broadcasted_iota(jnp.int32, (BLOCK, HALF), 0)
        feature = ((p // 32) % 8) * 128 + h * 64 + (p // 256) * 32 + p % 32
        pick = (f == feature).astype(F32).astype(BF16)
        rows = pl.ds(part * HALF, HALF)
        G[x, h, rows, :] = jnp.dot(a_ref[rows, :], pick, preferred_element_type=F32).astype(BF16)

    def turn(x_from, h, dst):
        r = lax.broadcasted_iota(jnp.int32, (HALF, HALF), 0)
        f = lax.broadcasted_iota(jnp.int32, (HALF, HALF), 1)
        one = (r == f).astype(F32).astype(BF16)
        dst[...] = lax.dot_general(one, G[x_from, h], LAST, preferred_element_type=F32).astype(BF16)

    def x_unit(x_, h, part):
        return G.at[x_, h, pl.ds(part * HALF, HALF), :]

    def x_send(d, step, x_, h, part):
        return send(x_unit(x_, h, part), x_unit(x_, h, part), xs.at[d, step], xr.at[d, step], x_dev[d])

    x_from = (x_prev, x_next)

    def x_arrived(d, step, h, part):
        arrived(x_unit(x_from[d], h, part), xs.at[d, step], xr.at[d, step])

    def h_of(x_):
        return x_ // 2

    low, high = pl.ds(0, W), pl.ds(W, HALF - W)

    def y_sends(k, slot):
        send(Q.at[0, slot, low], Q.at[1, slot, low], ys.at[k, 0], yr.at[k, 0], y_down)
        send(Q.at[0, slot, high], RL.at[k], ys.at[k, 2], yr.at[k, 2], y_up)
        send(Q.at[0, slot, high], Q.at[1, slot, high], ys.at[k, 1], yr.at[k, 1], y_down)

    def y_forward_down(k, slot):
        arrived(Q.at[1, slot, low], ys.at[k, 0], yr.at[k, 0])
        send(Q.at[1, slot, low], Q.at[2, slot, low], ys.at[k, 3], yr.at[k, 3], y_down)

    def y_forward_up(k, slot):
        arrived(RL.at[k], ys.at[k, 2], yr.at[k, 2])
        send(RL.at[k], Q.at[2, slot, high], ys.at[k, 4], yr.at[k, 4], y_up)

    slots = ((0, hi), (1, 1 - hi))
    far_lo = (lo + s) % 2
    cell_lo = (lo, lo, lo, lo, 1 - lo, lo, 1 - lo, 1 - lo, lo, far_lo, far_lo, 1 - lo)
    cell_h = (hi, 1 - hi, hi, 1 - hi, 0, hi, 0, 1, 1 - hi, hi, 1 - hi, 1)

    def compute(cell):
        rel, l, h = CELL_REL[cell], cell_lo[cell], cell_h[cell]

        @pl.loop(0, 2)
        def _(n):
            cols = pl.ds(pl.multiple_of(n * 256, 256), 256)
            if cell in OWN:
                rows = QP[...] if rel is None else Q[rel, hi]
                acc = jnp.dot(rows, G[x, h, :, cols], preferred_element_type=F32)
            else:
                acc = jnp.dot(Q[rel, 0], G[l, h, :, cols], preferred_element_type=F32)
                acc += jnp.dot(Q[rel, 1], G[2 + l, h, :, cols], preferred_element_type=F32)
            T[cell, :, :, :, cols] = acc.reshape(2, 8, ROWS, 256)

        send(T.at[cell, 1 - c], CR.at[cell], cs.at[cell], cr.at[cell], sibling)

    sides = (pl.ds(0, 256), pl.ds(256, 256))

    def z_landed(cell, d, step):
        part = ZR.at[cell, d, 0, :, sides[d]] if step == 0 else ZR.at[cell, d, step]
        arrived(part, zs.at[cell, d, step], zr.at[cell, d, step])

    def z_step(cell, step):
        if step == 0:
            arrived(CR.at[cell], cs.at[cell], cr.at[cell])
        for d in range(2):
            to = (z + 4 - step) % 8 if d == 0 else (z + 4 + step) % 8
            if step > 0:
                z_landed(cell, d, step - 1)
            if step == 0:
                cols = sides[d]
                T[cell, c, to, :, cols] = T[cell, c, to, :, cols] + CR[cell, to, :, cols]
                send(T.at[cell, c, to, :, cols], ZR.at[cell, d, 0, :, cols], zs.at[cell, d, 0], zr.at[cell, d, 0], z_dev[d])
                continue
            if step == 1:
                cols, rest = sides[d], sides[1 - d]
                T[cell, c, to, :, cols] = T[cell, c, to, :, cols] + CR[cell, to, :, cols] + ZR[cell, d, 0, :, cols]
                T[cell, c, to, :, rest] = T[cell, c, to, :, rest] + CR[cell, to, :, rest]
            else:
                T[cell, c, to] = T[cell, c, to] + CR[cell, to] + ZR[cell, d, step - 1]
            send(T.at[cell, c, to], ZR.at[cell, d, step], zs.at[cell, d, step], zr.at[cell, d, step], z_dev[d])

    def total(cell):
        z_landed(cell, 0, 3)
        z_landed(cell, 1, 3)
        return T[cell, c, z] + CR[cell, z] + ZR[cell, 0, 3] + ZR[cell, 1, 3]

    def natural(v):
        return scale * jnp.concatenate([v[h][:, k * 256 + b * 32:k * 256 + b * 32 + 32]
                                        for b in range(8) for h in range(2) for k in range(2)], axis=1)

    def out_cols(l, y_):
        return pl.ds(pl.multiple_of((l * 4 + y_) * BLOCK, BLOCK), BLOCK)

    def group(k):
        return pl.ds(pl.multiple_of(k * 256, 256), 256)

    mine_next, mine_far = lo * 4 + hi * 2 + c, 8 + hi * 2 + c

    def spread(cell):
        l, h = cell_lo[cell], cell_h[cell]
        R[cell] = total(cell)
        if cell in TO_FAR:
            send(R.at[cell], O2.at[h], ds.at[cell], dr.at[cell], at(x, y_far, z, c))
        else:
            send(R.at[cell], O1.at[l, h], ds.at[cell], dr.at[cell], y_up)
        mine = mine_far if cell in TO_FAR else mine_next
        for dk in range(2):
            k = (c + dk) % 2
            src, dev = R.at[cell, :, group(k)], at(2 * h + l, y, z, k)
            if dk or cell not in (5, 9):
                send(src, MB.at[mine], ms.at[cell, dk], mr.at[mine], dev)
            elif cell == 5:
                MB[mine] = R[cell, :, group(k)]
            else:
                @pl.when(s == 0)
                def _():
                    MB[mine] = R[cell, :, group(k)]

                @pl.when(s == 1)
                def _():
                    pltpu.make_async_remote_copy(
                        src_ref=src, dst_ref=MB.at[mine], send_sem=ms.at[cell, dk], recv_sem=mr.at[mine],
                        device_id=dev, device_id_type=MESH).start()

    def swap_own():
        for cell in (2, 3):
            R[cell] = total(cell)
            send(R.at[cell], PR.at[cell_h[cell]], ds.at[cell], dr.at[cell], at(x_opposite, y, z, c))

    mirror_base = ((1 - lo) * 4, lo * 4, 8)

    def mirror(b):
        for n in range(4):
            slot = mirror_base[b] + n
            if b == 0:
                arrived(MB.at[slot], ms.at[5, 0], mr.at[slot])
            else:
                @pl.when((n != hi * 2 + c) | ((s == 1) if b == 2 else False))
                def _():
                    arrived(MB.at[slot], ms.at[5, 0], mr.at[slot])
        if b == 2:
            @pl.when(s == 1)
            def _():
                pltpu.make_async_remote_copy(
                    src_ref=R.at[9, :, group(c)], dst_ref=MB.at[mine_far], send_sem=ms.at[9, 0], recv_sem=mr.at[mine_far],
                    device_id=sibling, device_id_type=MESH).wait_send()
        MT[b] = jnp.transpose(MB[pl.ds(mirror_base[b], 4)].reshape(4 * ROWS, 256)).reshape(8, ROWS, 4 * ROWS) * scale
        MO[b, z] = MT[b, z]
        for dz in range(1, 8):
            to = (z + dz) % 8
            send(MT.at[b, to], MO.at[b, z], ts.at[b, dz], tr.at[b, dz], at(x, y, to, c))

    stored = []

    def store(n, l, y_, v):
        OUT[n] = v
        cp = pltpu.make_async_copy(OUT.at[n], out_ref.at[:, out_cols(l, y_)], os.at[n])
        cp.start()
        stored.append(cp)

    def store_mirror(b, l, y_):
        for dz in range(1, 8):
            arrived(MO.at[b, (z + 8 - dz) % 8], ts.at[b, dz], tr.at[b, dz])
        store(5 + b, l, y_, jnp.concatenate([MO[b, k] for k in range(8)], axis=1))

    x_opposite = (x + 2) % 4
    for part in range(2):
        reorder(1 - hi, part)
    pl.semaphore_wait(barrier, len(partners))
    for part in range(2):
        x_send(part, 0, x, 1 - hi, part)
    for part in range(2):
        reorder(hi, part)
    turn(x, hi, Q.at[0, hi])
    y_sends(0, hi)
    compute(0)
    compute(1)
    z_step(0, 0)
    turn(x, 1 - hi, QP)
    compute(2)
    z_step(1, 0)
    z_step(0, 1)
    compute(3)
    z_step(2, 0)
    z_step(1, 1)
    z_step(0, 2)
    for d in range(2):
        x_arrived(d, 0, 1 - h_of(x_from[d]), d)
        x_send(d, 1, x_from[d], 1 - h_of(x_from[d]), d)
    z_step(3, 0)
    z_step(2, 1)
    z_step(1, 2)
    z_step(0, 3)
    y_forward_up(0, hi)
    z_step(3, 1)
    z_step(2, 2)
    z_step(1, 3)
    z_step(3, 2)
    z_step(2, 3)
    for d in range(2):
        arrived(x_unit(x_opposite, hi, d), xs.at[d, 1], xr.at[d, 1])
        x_send(d, 2, x, hi, d)
        x_send(d, 4, x, 0, 1 - d)
    turn(x_opposite, hi, Q.at[0, 1 - hi])
    y_sends(1, 1 - hi)
    z_step(3, 3)
    swap_own()
    y_forward_up(1, 1 - hi)
    for d in range(2):
        x_arrived(d, 2, h_of(x_from[d]), d)
        x_arrived(d, 4, 0, 1 - d)
        x_send(d, 5, x, 1, 1 - d)
        x_send(d, 3, x_from[d], h_of(x_from[d]), d)
    compute(4)
    for k, slot in slots:
        y_forward_down(k, slot)
        arrived(Q.at[1, slot, high], ys.at[k, 1], yr.at[k, 1])
    compute(5)
    compute(6)
    z_step(4, 0)
    z_step(5, 0)
    z_step(6, 0)
    z_step(4, 1)
    z_step(5, 1)
    z_step(6, 1)
    z_step(4, 2)
    z_step(5, 2)
    z_step(6, 2)
    z_step(4, 3)
    z_step(5, 3)
    z_step(6, 3)
    for d in range(2):
        x_arrived(d, 5, 1, 1 - d)
    for k, slot in slots:
        arrived(Q.at[2, slot, low], ys.at[k, 3], yr.at[k, 3])
        arrived(Q.at[2, slot, high], ys.at[k, 4], yr.at[k, 4])
    compute(9)
    compute(7)
    spread(5)
    spread(6)
    z_step(9, 0)
    for d in range(2):
        arrived(x_unit(x_opposite, 1 - hi, d), xs.at[d, 3], xr.at[d, 3])
    compute(8)
    compute(10)
    z_step(9, 1)
    z_step(7, 0)
    z_step(8, 0)
    z_step(10, 0)
    z_step(9, 2)
    z_step(7, 1)
    z_step(8, 1)
    z_step(10, 1)
    z_step(9, 3)
    compute(11)
    z_step(7, 2)
    z_step(8, 2)
    z_step(11, 0)
    z_step(10, 2)
    spread(9)
    z_step(7, 3)
    z_step(8, 3)
    z_step(11, 1)
    z_step(10, 3)
    spread(7)
    spread(8)
    mirror(0)
    z_step(11, 2)
    mirror(1)
    spread(10)
    mirror(2)
    z_step(11, 3)
    for cell in (2, 3):
        arrived(PR.at[1 - cell_h[cell]], ds.at[cell], dr.at[cell])
    first, second = total(0) + PR[hi], total(1) + PR[1 - hi]
    store(0, lo, y, natural((jnp.where(hi == 0, first, second), jnp.where(hi == 0, second, first))))
    for cell in TO_NEXT:
        arrived(O1.at[cell_lo[cell], cell_h[cell]], ds.at[cell], dr.at[cell])
    for l in range(2):
        store(1 + l, l, y_prev, natural(O1[l]))
    store_mirror(0, 1 - lo, y_next)
    for cell in TO_FAR:
        arrived(O2.at[cell_h[cell]], ds.at[cell], dr.at[cell])
    store(3, (lo + 1 - s) % 2, y_far, natural(O2[...]))
    store(4, 1 - lo, y, natural((total(4), total(11))))
    store_mirror(1, lo, y_next)
    store_mirror(2, far_lo, y_far)
    for cp in pending:
        cp.wait_send()
    for cp in stored:
        cp.wait()


def solution(mesh):
    token_ranks = mesh.shape["tok"]

    def shards(activations):
        scale = 1.0 / (activations.shape[0] * token_ranks)
        dma = pltpu.SemaphoreType.DMA
        return pl.pallas_call(
            lambda *refs: kernel(scale, *refs),
            out_shape=jax.ShapeDtypeStruct((ROWS, 8 * BLOCK), F32),
            in_specs=[pl.BlockSpec(memory_space=pltpu.VMEM)],
            out_specs=pl.BlockSpec(memory_space=pl.ANY),
            scratch_shapes=[
                pltpu.VMEM((4, 2, BLOCK, HALF), BF16),
                pltpu.VMEM((3, 2, HALF, BLOCK), BF16),
                pltpu.VMEM((HALF, BLOCK), BF16),
                pltpu.VMEM((2, HALF - W, BLOCK), BF16),
                pltpu.VMEM((CELLS, 2, 8, ROWS, HALF), F32),
                pltpu.VMEM((CELLS, 8, ROWS, HALF), F32),
                pltpu.VMEM((CELLS, 2, 4, ROWS, HALF), F32),
                pltpu.VMEM((CELLS, ROWS, HALF), F32),
                pltpu.VMEM((2, ROWS, HALF), F32),
                pltpu.VMEM((2, 2, ROWS, HALF), F32),
                pltpu.VMEM((2, ROWS, HALF), F32),
                pltpu.VMEM((12, ROWS, 256), F32),
                pltpu.VMEM((3, 8, ROWS, 4 * ROWS), F32),
                pltpu.VMEM((3, 8, ROWS, 4 * ROWS), F32),
                pltpu.VMEM((8, ROWS, BLOCK), F32),
                dma((2, 6)), dma((2, 6)),
                dma((2, 5)), dma((2, 5)),
                dma((CELLS,)), dma((CELLS,)),
                dma((CELLS, 2, 4)), dma((CELLS, 2, 4)),
                dma((CELLS,)), dma((CELLS,)),
                dma((CELLS, 2)), dma((12,)),
                dma((3, 8)), dma((3, 8)),
                dma((8,)),
            ],
            compiler_params=pltpu.CompilerParams(
                collective_id=0, has_side_effects=True, vmem_limit_bytes=56 * 1024 * 1024),
            cost_estimate=pl.CostEstimate(flops=14 * 10**9, bytes_accessed=3 * 2**20, transcendentals=0),
            name="gram",
        )(activations)

    return jax.shard_map(shards, mesh=mesh, in_specs=(P("tok", "col"),), out_specs=P(("col", "tok"), None), check_vma=False)
```

time: 142 us -> 132 us (0.930)
  Pallas kernels: 140 us -> 130 us
    pallas_call x1, Pallas kernels: 140 us -> 130 us  [shards(): pl.pallas_call(lambda *refs: kernel(scale, *refs), out_shape=jax.ShapeDty...]
where the time goes in v2:
time: 132 us
  Pallas kernels  130 us (98%)
  local copies, waits for them, and re-layouts  2.26 us (2%)
    pallas_call x1, Pallas kernels, shards(): pl.pallas_call(lambda *refs: kernel(scale, *refs), out_shape=jax.ShapeDty...  130 us

profile of v2, /device:TPU:1, one launch (start us, length us, event | category | flops | bytes accessed | tf_op | source)
XLA Modules:
  0.0 132.1 jit_solution(15425809485423664306)
XLA Ops:
  0.0 129.8 %gram.1 = f32[32,8192]{1,0:T(8,128)} custom-call(bf16[1024,1024]{1,0:T(8,128)(2,1)} %refs_0_.1), custom_call_target="tpu_custom_call" | custom-call | flops 14000000000 | bytes 3145728 | tf_op jit(solution)/shard_map/gram/pallas_call | solution.py:368
  129.8 2.3 %copy.3 = f32[32,8192]{1,0:T(8,128)} copy(f32[32,8192]{1,0:T(8,128)} %gram.1) | data formatting | bytes 2097152

commit v3 on v0

v3 whole, which is shorter than its diff:
```python
import jax
import jax.numpy as jnp
from jax import lax
from jax.experimental import pallas as pl
from jax.experimental.pallas import tpu as pltpu
from jax.sharding import PartitionSpec as P

MESH = pl.DeviceIdType.MESH
F32, BF16 = jnp.float32, jnp.bfloat16
BLOCK = 1024
HALF = BLOCK // 2
CH = HALF // 2
ROWS = 32
PART = ROWS // 2
W = 80
LAST = (((1,), (1,)), ((), ()))
A, B = 0, 1
OWN, PEER, SELF, NEXT, FAR = range(5)
CELLS = (
    ((OWN, A, "p", A), (OWN, A, "p", B)),
    ((OWN, A, "r", A), (OWN, A, "r", B)),
    ((OWN, B, "p", A), (OWN, B, "p", B)),
    ((OWN, B, "r", A), (OWN, B, "r", B)),
    ((PEER, A, "p", A), (PEER, A, "p", B)),
    ((PEER, A, "r", A), (PEER, A, "r", B)),
    ((PEER, B, "p", A), (PEER, B, "p", B)),
    ((PEER, B, "r", A), (PEER, B, "r", B)),
    ((SELF, A, "1", A), (NEXT, A, "1", A)),
    ((NEXT, A, "r", B), (NEXT, B, "r", B)),
    ((NEXT, A, "p", B), (NEXT, A, "p", A)),
    ((SELF, A, "1", B), (SELF, B, "1", B)),
    ((SELF, A, "0", A), (SELF, B, "0", A)),
    ((SELF, B, "1", A), (NEXT, A, "0", A)),
    ((NEXT, A, "0", B), (SELF, B, "0", B)),
    ((FAR, B, "f", A), (FAR, B, "g", A)),
    ((NEXT, B, "1", A), (NEXT, B, "r", A)),
    ((NEXT, A, "r", A), (NEXT, B, "p", B)),
    ((FAR, A, "f", A), (FAR, A, "g", A)),
    ((FAR, A, "f", B), (FAR, A, "g", B)),
    ((SELF, A, "0", B), (NEXT, B, "0", B)),
    ((NEXT, A, "1", B), (NEXT, B, "1", B)),
    ((NEXT, B, "0", A), (NEXT, B, "p", A)),
    ((FAR, B, "g", B), (FAR, B, "f", B)),
)
COUNT = len(CELLS)
X_NEEDS = {("p", A): (1,), ("p", B): (3,), ("r", A): (7,), ("r", B): (11,), ("0", A): (0, 4, 5), ("0", B): (2, 8, 9),
           ("1", A): (0, 4, 6), ("1", B): (2, 8, 10), ("f", A): (1, 0, 4, 5, 6), ("f", B): (3, 2, 8, 9, 10),
           ("g", A): (7, 0, 4, 5, 6), ("g", B): (11, 2, 8, 9, 10)}
ORDER = (
    ('c', 0), ('c', 1), ('c', 2), ('c', 3), ('c', 4), ('c', 5), ('c', 6), ('z', 0, 0),
    ('z', 1, 0), ('x', 1), ('z', 2, 0), ('z', 3, 0), ('z', 4, 0), ('z', 5, 0), ('z', 6, 0), ('z', 0, 1),
    ('z', 1, 1), ('z', 2, 1), ('z', 3, 1), ('z', 4, 1), ('y', 0, 0, 4), ('z', 5, 1), ('z', 6, 1), ('z', 0, 2),
    ('z', 1, 2), ('z', 2, 2), ('x', 2), ('z', 3, 2), ('z', 4, 2), ('z', 5, 2), ('z', 6, 2), ('z', 0, 3),
    ('c', 7), ('z', 1, 3), ('z', 2, 3), ('z', 3, 3), ('z', 4, 3), ('z', 7, 0), ('z', 5, 3), ('z', 6, 3),
    ('f', 0), ('f', 1), ('f', 2), ('f', 3), ('f', 4), ('x', 3), ('z', 7, 1), ('f', 5),
    ('f', 6), ('y', 1, 0, 4), ('z', 7, 2), ('z', 7, 3), ('f', 7), ('y', 0, 1, 4), ('x', 4), ('c', 10),
    ('c', 12), ('z', 10, 0), ('z', 12, 0), ('c', 8), ('z', 10, 1), ('c', 13), ('z', 12, 1), ('z', 8, 0),
    ('z', 10, 2), ('z', 13, 0), ('z', 12, 2), ('z', 8, 1), ('z', 10, 3), ('z', 13, 1), ('y', 0, 0, 3), ('y', 1, 0, 3),
    ('y', 0, 1, 3), ('y', 1, 1, 3), ('c', 16), ('z', 12, 3), ('c', 17), ('z', 8, 2), ('c', 22), ('f', 10),
    ('z', 13, 2), ('z', 16, 0), ('f', 12), ('x', 5), ('z', 17, 0), ('z', 8, 3), ('z', 22, 0), ('z', 13, 3),
    ('z', 16, 1), ('z', 17, 1), ('f', 8), ('z', 22, 1), ('c', 18), ('f', 13), ('y', 1, 1, 4), ('z', 16, 2),
    ('c', 14), ('z', 17, 2), ('c', 20), ('z', 18, 0), ('z', 22, 2), ('z', 16, 3), ('z', 14, 0), ('z', 17, 3),
    ('z', 20, 0), ('z', 18, 1), ('z', 22, 3), ('f', 16), ('c', 11), ('z', 14, 1), ('c', 21), ('z', 20, 1),
    ('f', 17), ('z', 18, 2), ('f', 22), ('c', 15), ('z', 11, 0), ('z', 14, 2), ('z', 21, 0), ('z', 20, 2),
    ('z', 18, 3), ('c', 9), ('z', 11, 1), ('z', 15, 0), ('c', 19), ('z', 14, 3), ('z', 21, 1), ('c', 23),
    ('z', 20, 3), ('f', 18), ('z', 9, 0), ('m', 0, 0), ('z', 11, 2), ('m', 1, 0), ('z', 15, 1), ('z', 19, 0),
    ('f', 14), ('z', 23, 0), ('z', 21, 2), ('f', 20), ('z', 9, 1), ('z', 11, 3), ('z', 15, 2), ('z', 19, 1),
    ('z', 23, 1), ('z', 21, 3), ('z', 9, 2), ('f', 11), ('own',), ('self',), ('z', 15, 3), ('z', 19, 2),
    ('z', 23, 2), ('f', 21), ('z', 9, 3), ('f', 15), ('z', 19, 3), ('z', 23, 3), ('m', 0, 1), ('f', 9),
    ('m', 2, 0), ('f', 19), ('f', 23), ('m', 1, 1), ('next',), ('m', 2, 1), ('far',),
)


def kernel(scale, a_ref, out_ref, G, Q, QP, RL, T, CR, ZR, R, PR, D, O1, O2, MB, MT, MO, OUT,
           xs, xr, ys, yr, cs, cr, zs, zr, ds, dr, ms, mr, ts, tr, os):
    col, tok = lax.axis_index("col"), lax.axis_index("tok")
    lo, y = col // 4, col % 4
    z, hi, c = tok // 4, (tok // 2) % 2, tok % 2
    x = 2 * hi + lo
    s = y // 2

    def at(x_, y_, z_, c_):
        return ((x_ % 2) * 4 + y_, z_ * 4 + (x_ // 2) * 2 + c_)

    x_next, x_prev, x_opposite = (x + 1) % 4, (x + 3) % 4, (x + 2) % 4
    y_next, y_prev, y_far = (y + 1) % 4, (y + 3) % 4, (y + 2) % 4
    x_dev = (at(x_next, y, z, c), at(x_prev, y, z, c))
    x_from = (x_prev, x_next)
    y_up, y_down = at(x, y_next, z, c), at(x, y_prev, z, c)
    sibling = at(x, y, z, 1 - c)
    z_dev = (at(x, y, (z + 1) % 8, c), at(x, y, (z + 7) % 8, c))
    far_lo = (lo + s) % 2
    half_lo = {"p": lo, "r": lo, "0": 1 - lo, "1": 1 - lo, "f": far_lo, "g": far_lo}
    half_h = {"p": hi, "r": 1 - hi, "0": 0, "1": 1, "f": hi, "g": 1 - hi}

    def send(src, dst, s_sem, r_sem, dev):
        cp = pltpu.make_async_remote_copy(src_ref=src, dst_ref=dst, send_sem=s_sem, recv_sem=r_sem,
                                          device_id=dev, device_id_type=MESH)
        cp.start()

    def taken(ref, sem):
        pltpu.make_async_copy(ref, ref, sem).wait()

    partners = [at(2 * (hi ^ dh) + (lo ^ dl), y, z, c ^ dc)
                for dh in range(2) for dl in range(2) for dc in range(2) if dh + dl + dc]
    partners += [at(x, y, (z + dz) % 8, c) for dz in range(1, 8)]
    partners += [at(x, (y + dy) % 4, z, c) for dy in range(1, 4)]
    barrier = pltpu.get_barrier_semaphore()
    for dev in partners:
        pl.semaphore_signal(barrier, inc=1, device_id=dev, device_id_type=MESH)

    def reorder(h, part):
        p = lax.broadcasted_iota(jnp.int32, (BLOCK, HALF), 1)
        f = lax.broadcasted_iota(jnp.int32, (BLOCK, HALF), 0)
        feature = ((p // PART) % 8) * 128 + h * 64 + ((p // 128) % 2) * 32 + (p // CH) * PART + p % PART
        pick = (f == feature).astype(F32).astype(BF16)
        rows = pl.ds(part * HALF, HALF)
        v = jnp.dot(a_ref[rows, :], pick, preferred_element_type=F32).astype(BF16)
        for cc in (A, B):
            G[x, h, cc, rows, :] = v[:, cc * CH:cc * CH + CH]

    def turn(x_, h, cc, dst):
        r = lax.broadcasted_iota(jnp.int32, (CH, CH), 0)
        f = lax.broadcasted_iota(jnp.int32, (CH, CH), 1)
        one = (r == f).astype(F32).astype(BF16)
        dst[...] = lax.dot_general(one, G[x_, h, cc], LAST, preferred_element_type=F32).astype(BF16)

    def h_of(x_):
        return x_ // 2

    def x_sent(n, d):
        b = x_from[d]
        return {0: (x, 1 - hi, A, d), 1: (b, 1 - h_of(b), A, d), 2: (x, 1 - hi, B, d), 3: (b, 1 - h_of(b), B, d),
                4: (x, hi, A, d), 5: (x, 0, A, 1 - d), 6: (x, 1, A, 1 - d), 7: (b, h_of(b), A, d),
                8: (x, hi, B, d), 9: (x, 0, B, 1 - d), 10: (x, 1, B, 1 - d), 11: (b, h_of(b), B, d)}[n]

    def x_unit(x_, h, cc, part):
        return G.at[x_, h, cc, pl.ds(part * HALF, HALF), :]

    def x_send(*messages):
        for n in messages:
            for d in range(2):
                u = x_unit(*x_sent(n, d))
                send(u, u, xs.at[0], xr.at[n], x_dev[d])

    low, high = pl.ds(0, W), pl.ds(W, CH - W)
    slots = (hi, 1 - hi)

    def y_landing(k, r, m):
        q = slots[k]
        return (Q.at[1, q, r, low], Q.at[1, q, r, high], RL.at[2 * k + r], Q.at[2, q, r, low], Q.at[2, q, r, high])[m]

    def y_send(k, r, *messages):
        for m in messages:
            q = slots[k]
            src = (Q.at[0, q, r, low], Q.at[0, q, r, high], Q.at[0, q, r, high], Q.at[1, q, r, low], RL.at[2 * k + r])[m]
            send(src, y_landing(k, r, m), ys.at[m], yr.at[2 * k + r, m], y_down if m in (0, 1, 3) else y_up)

    waited = set()

    def need_x(*messages):
        for n in messages:
            if ("x", n) not in waited:
                waited.add(("x", n))
                taken(G.at[0, 0, 0], xr.at[n])

    def need_y(k, r, *messages):
        for m in messages:
            if ("y", k, r, m) not in waited:
                waited.add(("y", k, r, m))
                taken(y_landing(k, r, m), yr.at[2 * k + r, m])

    def x_step(n):
        if n == 1:
            need_x(0)
            x_send(1, 4, 2, 5)
        elif n == 2:
            need_x(1)
            turn(x_opposite, hi, A, Q.at[0, 1 - hi, A])
            y_send(1, A, 0, 2, 1)
            y_send(0, B, 0, 2, 1)
        elif n == 3:
            need_x(2, 4)
            x_send(3, 6, 7, 8, 9, 10)
        elif n == 4:
            need_x(3)
            turn(x_opposite, hi, B, Q.at[0, 1 - hi, B])
            y_send(1, B, 0, 2, 1)
        else:
            need_x(8)
            x_send(11)

    def y_step(k, r, m):
        need_y(k, r, 0 if m == 3 else 2)
        y_send(k, r, m)

    def compute(cell):
        for j, (kind, r, half, cc) in enumerate(CELLS[cell]):
            l, h = half_lo[half], half_h[half]
            if kind in (OWN, PEER):
                rows = QP[r] if kind == PEER else Q[0, hi, r]
                acc = jnp.dot(rows, G[x, h, cc], preferred_element_type=F32)
            else:
                need_x(*X_NEEDS[half, cc])
                for k in range(2):
                    need_y(k, r, *((), (0, 1), (3, 4))[kind - SELF])
                acc = jnp.dot(Q[kind - SELF, 0, r], G[l, h, cc], preferred_element_type=F32)
                acc += jnp.dot(Q[kind - SELF, 1, r], G[2 + l, h, cc], preferred_element_type=F32)
            T[cell, :, :, :, j * CH:j * CH + CH] = acc.reshape(2, 8, PART, CH)
        send(T.at[cell, 1 - c], CR.at[cell], cs.at[0], cr.at[cell], sibling)

    sides = (pl.ds(0, CH), pl.ds(CH, CH))

    def z_landed(cell, step):
        taken(ZR.at[cell, :, step] if step else ZR.at[cell, 0, 0], zr.at[cell, step])

    def z_step(cell, step):
        if step == 0:
            taken(CR.at[cell], cr.at[cell])
        else:
            z_landed(cell, step - 1)
        for d in range(2):
            to = (z + 4 - step) % 8 if d == 0 else (z + 4 + step) % 8
            if step == 0:
                cols = sides[d]
                T[cell, c, to, :, cols] = T[cell, c, to, :, cols] + CR[cell, to, :, cols]
                send(T.at[cell, c, to, :, cols], ZR.at[cell, d, 0, :, cols], zs.at[0], zr.at[cell, 0], z_dev[d])
                continue
            if step == 1:
                cols, rest = sides[d], sides[1 - d]
                T[cell, c, to, :, cols] = T[cell, c, to, :, cols] + CR[cell, to, :, cols] + ZR[cell, d, 0, :, cols]
                T[cell, c, to, :, rest] = T[cell, c, to, :, rest] + CR[cell, to, :, rest]
            else:
                T[cell, c, to] = T[cell, c, to] + CR[cell, to] + ZR[cell, d, step - 1]
            send(T.at[cell, c, to], ZR.at[cell, d, step], zs.at[0], zr.at[cell, step], z_dev[d])

    def out_cols(l, y_):
        return pl.ds(pl.multiple_of((l * 4 + y_) * BLOCK, BLOCK), BLOCK)

    def group(j, k):
        return pl.ds(pl.multiple_of(j * CH + k * 128, 128), 128)

    def mirror_self(half, k):
        return "no" if k else {"p": "yes", "f": "some"}.get(half, "no")

    def finish(cell):
        z_landed(cell, 3)
        R[cell] = T[cell, c, z] + CR[cell, z] + ZR[cell, 0, 3] + ZR[cell, 1, 3]
        for j, (kind, r, half, cc) in enumerate(CELLS[cell]):
            l, h = half_lo[half], half_h[half]
            cols = pl.ds(j * CH, CH)
            src = R.at[cell, :, cols]
            if kind in (OWN, SELF):
                D[l, h, cc, r] = R[cell, :, cols]
                continue
            if kind == PEER:
                send(src, PR.at[h, cc, r], ds.at[0], dr.at[0], at(x_opposite, y, z, c))
                continue
            if kind == NEXT:
                send(src, O1.at[l, h, cc, r], ds.at[1], dr.at[1], y_up)
            else:
                send(src, O2.at[h, cc, r], ds.at[2], dr.at[2], at(x, y_far, z, c))
            mine = (8 if kind == FAR else lo * 4) + hi * 2 + c
            s_sem, batch = ms.at[kind - NEXT], 2 if kind == FAR else 1 if half in "pr" else 0
            for dk in range(2):
                k = (c + dk) % 2
                part, dst, dev = R.at[cell, :, group(j, k)], MB.at[cc, mine, r], at(2 * h + l, y, z, k)
                stays = mirror_self(half, dk)

                def leave():
                    send(part, dst, s_sem, mr.at[batch, cc], dev)

                def keep():
                    MB[cc, mine, r] = R[cell, :, group(j, k)]
                if stays == "no":
                    leave()
                elif stays == "yes":
                    keep()
                else:
                    pl.when(s == 0)(keep)
                    pl.when(s == 1)(leave)

    mirror_base = ((1 - lo) * 4, lo * 4, 8)

    def mirror(b, cc):
        def take(n):
            taken(MB.at[cc, 0:n], mr.at[b, cc])
        if b < 2:
            take(4 - b)
        else:
            pl.when(s == 0)(lambda: take(3))
            pl.when(s == 1)(lambda: take(4))
        turned = jnp.transpose(MB[cc, pl.ds(mirror_base[b], 4)].reshape(4 * ROWS, 4 * ROWS))
        MT[b, cc] = turned.reshape(8, PART, 4 * ROWS) * scale
        MO[b, z, cc] = MT[b, cc, z]
        for dz in range(1, 8):
            to = (z + dz) % 8
            send(MT.at[b, cc, to], MO.at[b, z, cc], ts.at[0], tr.at[b, cc], at(x, y, to, c))

    def store(n, l, y_, v):
        OUT[n] = v
        pltpu.make_async_copy(OUT.at[n], out_ref.at[:, out_cols(l, y_)], os.at[0]).start()

    def natural(v):
        t = [[v[h, cc].reshape(ROWS, CH) for cc in (A, B)] for h in range(2)]
        return scale * jnp.concatenate([t[h][cc][:, k * 128 + b * PART:k * 128 + b * PART + PART]
                                        for b in range(8) for h in range(2) for k in range(2) for cc in (A, B)], axis=1)

    def store_mirror(b, l, y_):
        for cc in (A, B):
            taken(MO.at[b, 0:7, cc], tr.at[b, cc])
        store(5 + b, l, y_, jnp.concatenate([MO[b, k].reshape(ROWS, 4 * ROWS) for k in range(8)], axis=1))

    def store_own():
        taken(PR, dr.at[0])
        store(0, lo, y, natural(D[lo] + PR[...]))

    def store_next():
        taken(O1, dr.at[1])
        for l in range(2):
            store(1 + l, l, y_prev, natural(O1[l]))

    def store_far():
        taken(O2, dr.at[2])
        store(3, (lo + 1 - s) % 2, y_far, natural(O2[...]))

    def store_self():
        store(4, 1 - lo, y, natural(D[1 - lo]))

    for part in range(2):
        reorder(1 - hi, part)
    pl.semaphore_wait(barrier, len(partners))
    x_send(0)
    for part in range(2):
        reorder(hi, part)
    turn(x, hi, A, Q.at[0, hi, A])
    y_send(0, A, 0, 2, 1)
    turn(x, hi, B, Q.at[0, hi, B])
    for cc in (A, B):
        turn(x, 1 - hi, cc, QP.at[cc])

    steps = {"x": x_step, "y": y_step, "c": compute, "z": z_step, "f": finish, "m": mirror, "own": store_own, "next": store_next,
             "far": store_far, "self": store_self}
    for name, *given in ORDER:
        steps[name](*given)
    store_mirror(0, 1 - lo, y_next)
    store_mirror(1, lo, y_next)
    store_mirror(2, far_lo, y_far)

    taken(G.at[0:3], xs.at[0])
    for m in range(5):
        taken(Q.at[0, :, :, low if m in (0, 3) else high], ys.at[m])
    taken(CR, cs.at[0])
    taken(CR.at[0:COUNT * 7 // 8], zs.at[0])
    for n, ref in enumerate((PR, O1, O2)):
        taken(ref, ds.at[n])
    taken(MB.at[:, 0:7], ms.at[0])
    for v in range(2):
        pl.when(s == v)(lambda: taken(MB.at[:, 0:3 + v], ms.at[1]))
    taken(MT.at[:, :, 0:7], ts.at[0])
    taken(OUT, os.at[0])


def solution(mesh):
    token_ranks = mesh.shape["tok"]

    def shards(activations):
        scale = 1.0 / (activations.shape[0] * token_ranks)
        dma = pltpu.SemaphoreType.DMA
        return pl.pallas_call(
            lambda *refs: kernel(scale, *refs),
            out_shape=jax.ShapeDtypeStruct((ROWS, 8 * BLOCK), F32),
            in_specs=[pl.BlockSpec(memory_space=pltpu.VMEM)],
            out_specs=pl.BlockSpec(memory_space=pl.ANY),
            scratch_shapes=[
                pltpu.VMEM((4, 2, 2, BLOCK, CH), BF16),
                pltpu.VMEM((3, 2, 2, CH, BLOCK), BF16),
                pltpu.VMEM((2, CH, BLOCK), BF16),
                pltpu.VMEM((4, CH - W, BLOCK), BF16),
                pltpu.VMEM((COUNT, 2, 8, PART, HALF), F32),
                pltpu.VMEM((COUNT, 8, PART, HALF), F32),
                pltpu.VMEM((COUNT, 2, 4, PART, HALF), F32),
                pltpu.VMEM((COUNT, PART, HALF), F32),
                pltpu.VMEM((2, 2, 2, PART, CH), F32),
                pltpu.VMEM((2, 2, 2, 2, PART, CH), F32),
                pltpu.VMEM((2, 2, 2, 2, PART, CH), F32),
                pltpu.VMEM((2, 2, 2, PART, CH), F32),
                pltpu.VMEM((2, 12, 2, PART, 4 * ROWS), F32),
                pltpu.VMEM((3, 2, 8, PART, 4 * ROWS), F32),
                pltpu.VMEM((3, 8, 2, PART, 4 * ROWS), F32),
                pltpu.VMEM((8, ROWS, BLOCK), F32),
                dma((1,)), dma((12,)),
                dma((5,)), dma((4, 5)),
                dma((1,)), dma((COUNT,)),
                dma((1,)), dma((COUNT, 4)),
                dma((3,)), dma((3,)),
                dma((2,)), dma((3, 2)),
                dma((1,)), dma((3, 2)),
                dma((1,)),
            ],
            compiler_params=pltpu.CompilerParams(
                collective_id=0, has_side_effects=True, vmem_limit_bytes=56 * 1024 * 1024),
            cost_estimate=pl.CostEstimate(flops=14 * 10**9, bytes_accessed=3 * 2**20, transcendentals=0),
            name="gram",
        )(activations)

    return jax.shard_map(shards, mesh=mesh, in_specs=(P("tok", "col"),), out_specs=P(("col", "tok"), None), check_vma=False)
```

time: 725 us -> 127 us (0.18)
  waiting for transfers between devices: 603 us -> 0 us
  Pallas kernels: 0 us -> 123 us
  starting transfers between devices: 57.7 us -> 0 us
  matrix products: 23.4 us -> 0 us
  local copies, waits for them, and re-layouts: 20.5 us -> 2.26 us
  between operations: 13.5 us -> 0.01 us
    reduce_scatter x5 -> x0, waiting for transfers between devices: 407 us -> none  [shards(): lax.psum_scatter(make_term(left_block, right_block), 'tok', scatter_dimen...]
    ppermute x7 -> x0, waiting for transfers between devices: 181 us -> none  [passed_along(): lax.ppermute(value, axis, [(i, (i + by) % size) for i in range(size)])]
    pallas_call x0 -> x1, Pallas kernels: none -> 123 us  [shards(): pl.pallas_call(lambda *refs: kernel(scale, *refs), out_shape=jax.ShapeDty...]
    all_to_all x3 -> x0, starting transfers between devices: 33.4 us -> none  [shards(): lax.all_to_all(reduced_tile, 'tok', split_axis=1, concat_axis=0, tiled=True)]
    ppermute x7 -> x0, starting transfers between devices: 24.1 us -> none  [passed_along(): lax.ppermute(value, axis, [(i, (i + by) % size) for i in range(size)])]
    dot_general x5 -> x0, matrix products: 23.4 us -> none  [make_term(): lax.dot_general(left_block, right_block, contract_first, preferred_elemen...]
    all_to_all x3 -> x0, waiting for transfers between devices: 15 us -> none  [shards(): lax.all_to_all(reduced_tile, 'tok', split_axis=1, concat_axis=0, tiled=True)]
    unnamed x39 -> x1, local copies, waits for them, and re-layouts: 11.7 us -> 2.26 us
  transfers between devices with their start and end apart: 15 -> 0, of which waited for: 10 -> 0; matrix products, arithmetic and copies ran while one was open for 4% -> 0% of each run, Pallas kernels for 0% -> 0%
where the time goes in v3:
time: 127 us; the launch traced here: 125 us
  Pallas kernels  123 us (97%)
  local copies, waits for them, and re-layouts  2.26 us (2%)
    pallas_call x1, Pallas kernels, shards(): pl.pallas_call(lambda *refs: kernel(scale, *refs), out_shape=jax.ShapeDty...  123 us

profile of v3, /device:TPU:1, one launch (start us, length us, event | category | flops | bytes accessed | tf_op | source)
XLA Modules:
  0.0 125.2 jit_solution(6394999173194663399)
XLA Ops:
  0.0 122.9 %gram.1 = f32[32,8192]{1,0:T(8,128)} custom-call(bf16[1024,1024]{1,0:T(8,128)(2,1)} %refs_0_.1), custom_call_target="tpu_custom_call" | custom-call | flops 14000000000 | bytes 3145728 | tf_op jit(solution)/shard_map/gram/pallas_call | solution.py:370
  122.9 2.3 %copy.3 = f32[32,8192]{1,0:T(8,128)} copy(f32[32,8192]{1,0:T(8,128)} %gram.1) | data formatting | bytes 2097152

commit v4 on v3

--- a/solution.py
+++ b/solution.py
@@ -17,61 +17,74 @@
 A, B = 0, 1
 OWN, PEER, SELF, NEXT, FAR = range(5)
 CELLS = (
-    ((OWN, A, "p", A), (OWN, A, "p", B)),
-    ((OWN, A, "r", A), (OWN, A, "r", B)),
-    ((OWN, B, "p", A), (OWN, B, "p", B)),
-    ((OWN, B, "r", A), (OWN, B, "r", B)),
-    ((PEER, A, "p", A), (PEER, A, "p", B)),
-    ((PEER, A, "r", A), (PEER, A, "r", B)),
-    ((PEER, B, "p", A), (PEER, B, "p", B)),
-    ((PEER, B, "r", A), (PEER, B, "r", B)),
-    ((SELF, A, "1", A), (NEXT, A, "1", A)),
-    ((NEXT, A, "r", B), (NEXT, B, "r", B)),
-    ((NEXT, A, "p", B), (NEXT, A, "p", A)),
-    ((SELF, A, "1", B), (SELF, B, "1", B)),
-    ((SELF, A, "0", A), (SELF, B, "0", A)),
-    ((SELF, B, "1", A), (NEXT, A, "0", A)),
-    ((NEXT, A, "0", B), (SELF, B, "0", B)),
-    ((FAR, B, "f", A), (FAR, B, "g", A)),
-    ((NEXT, B, "1", A), (NEXT, B, "r", A)),
-    ((NEXT, A, "r", A), (NEXT, B, "p", B)),
-    ((FAR, A, "f", A), (FAR, A, "g", A)),
-    ((FAR, A, "f", B), (FAR, A, "g", B)),
-    ((SELF, A, "0", B), (NEXT, B, "0", B)),
-    ((NEXT, A, "1", B), (NEXT, B, "1", B)),
-    ((NEXT, B, "0", A), (NEXT, B, "p", A)),
-    ((FAR, B, "g", B), (FAR, B, "f", B)),
+    ((OWN, A, "p", A), (OWN, A, "p", B),),
+    ((OWN, A, "r", A), (OWN, A, "r", B),),
+    ((OWN, B, "p", A), (OWN, B, "p", B),),
+    ((OWN, B, "r", A), (OWN, B, "r", B),),
+    ((PEER, A, "p", A), (PEER, A, "p", B),),
+    ((PEER, A, "r", A), (PEER, A, "r", B),),
+    ((PEER, B, "p", A), (PEER, B, "p", B),),
+    ((PEER, B, "r", A), (PEER, B, "r", B),),
+    ((FAR, B, "g", A),),
+    ((NEXT, A, "r", B), (FAR, B, "f", B),),
+    ((SELF, B, "u", B), (NEXT, B, "r", A),),
+    ((NEXT, A, "p", A),),
+    ((NEXT, A, "1", B), (NEXT, A, "r", A),),
+    ((SELF, B, "u", A),),
+    ((NEXT, B, "1", B),),
+    ((SELF, A, "u", B), (FAR, A, "f", B),),
+    ((NEXT, B, "p", B), (NEXT, B, "1", A),),
+    ((NEXT, B, "r", B),),
+    ((NEXT, A, "1", A), (NEXT, A, "p", B),),
+    ((FAR, A, "g", B),),
+    ((FAR, A, "g", A),),
+    ((FAR, A, "f", A),),
+    ((FAR, B, "g", B),),
+    ((NEXT, B, "p", A),),
+    ((FAR, B, "f", A),),
+    ((SELF, A, "u", A), (NEXT, A, "0", B),),
+    ((NEXT, A, "0", A), (NEXT, B, "0", A),),
+    ((NEXT, B, "0", B),),
 )
 COUNT = len(CELLS)
+PAIRS = sum(len(tiles) for tiles in CELLS) // 2
 X_NEEDS = {("p", A): (1,), ("p", B): (3,), ("r", A): (7,), ("r", B): (11,), ("0", A): (0, 4, 5), ("0", B): (2, 8, 9),
            ("1", A): (0, 4, 6), ("1", B): (2, 8, 10), ("f", A): (1, 0, 4, 5, 6), ("f", B): (3, 2, 8, 9, 10),
-           ("g", A): (7, 0, 4, 5, 6), ("g", B): (11, 2, 8, 9, 10)}
+           ("g", A): (7, 0, 4, 5, 6), ("g", B): (11, 2, 8, 9, 10), ("u", A): (0, 4, 5, 6), ("u", B): (2, 8, 9, 10)}
+X_FORWARD = {1: 0, 3: 2, 7: 4, 11: 8}
+X_GROUPS = ((0, 2), (1, 6, 5), (3, 4, 8, 9, 10), (7,), (11,))
+OWN_FIRST = True
+
 ORDER = (
     ('c', 0), ('c', 1), ('c', 2), ('c', 3), ('c', 4), ('c', 5), ('c', 6), ('z', 0, 0),
-    ('z', 1, 0), ('x', 1), ('z', 2, 0), ('z', 3, 0), ('z', 4, 0), ('z', 5, 0), ('z', 6, 0), ('z', 0, 1),
-    ('z', 1, 1), ('z', 2, 1), ('z', 3, 1), ('z', 4, 1), ('y', 0, 0, 4), ('z', 5, 1), ('z', 6, 1), ('z', 0, 2),
-    ('z', 1, 2), ('z', 2, 2), ('x', 2), ('z', 3, 2), ('z', 4, 2), ('z', 5, 2), ('z', 6, 2), ('z', 0, 3),
-    ('c', 7), ('z', 1, 3), ('z', 2, 3), ('z', 3, 3), ('z', 4, 3), ('z', 7, 0), ('z', 5, 3), ('z', 6, 3),
-    ('f', 0), ('f', 1), ('f', 2), ('f', 3), ('f', 4), ('x', 3), ('z', 7, 1), ('f', 5),
-    ('f', 6), ('y', 1, 0, 4), ('z', 7, 2), ('z', 7, 3), ('f', 7), ('y', 0, 1, 4), ('x', 4), ('c', 10),
-    ('c', 12), ('z', 10, 0), ('z', 12, 0), ('c', 8), ('z', 10, 1), ('c', 13), ('z', 12, 1), ('z', 8, 0),
-    ('z', 10, 2), ('z', 13, 0), ('z', 12, 2), ('z', 8, 1), ('z', 10, 3), ('z', 13, 1), ('y', 0, 0, 3), ('y', 1, 0, 3),
-    ('y', 0, 1, 3), ('y', 1, 1, 3), ('c', 16), ('z', 12, 3), ('c', 17), ('z', 8, 2), ('c', 22), ('f', 10),
-    ('z', 13, 2), ('z', 16, 0), ('f', 12), ('x', 5), ('z', 17, 0), ('z', 8, 3), ('z', 22, 0), ('z', 13, 3),
-    ('z', 16, 1), ('z', 17, 1), ('f', 8), ('z', 22, 1), ('c', 18), ('f', 13), ('y', 1, 1, 4), ('z', 16, 2),
-    ('c', 14), ('z', 17, 2), ('c', 20), ('z', 18, 0), ('z', 22, 2), ('z', 16, 3), ('z', 14, 0), ('z', 17, 3),
-    ('z', 20, 0), ('z', 18, 1), ('z', 22, 3), ('f', 16), ('c', 11), ('z', 14, 1), ('c', 21), ('z', 20, 1),
-    ('f', 17), ('z', 18, 2), ('f', 22), ('c', 15), ('z', 11, 0), ('z', 14, 2), ('z', 21, 0), ('z', 20, 2),
-    ('z', 18, 3), ('c', 9), ('z', 11, 1), ('z', 15, 0), ('c', 19), ('z', 14, 3), ('z', 21, 1), ('c', 23),
-    ('z', 20, 3), ('f', 18), ('z', 9, 0), ('m', 0, 0), ('z', 11, 2), ('m', 1, 0), ('z', 15, 1), ('z', 19, 0),
-    ('f', 14), ('z', 23, 0), ('z', 21, 2), ('f', 20), ('z', 9, 1), ('z', 11, 3), ('z', 15, 2), ('z', 19, 1),
-    ('z', 23, 1), ('z', 21, 3), ('z', 9, 2), ('f', 11), ('own',), ('self',), ('z', 15, 3), ('z', 19, 2),
-    ('z', 23, 2), ('f', 21), ('z', 9, 3), ('f', 15), ('z', 19, 3), ('z', 23, 3), ('m', 0, 1), ('f', 9),
-    ('m', 2, 0), ('f', 19), ('f', 23), ('m', 1, 1), ('next',), ('m', 2, 1), ('far',),
+    ('c', 7), ('z', 1, 0), ('z', 2, 0), ('x', 1), ('z', 3, 0), ('z', 4, 0), ('z', 5, 0), ('z', 6, 0),
+    ('z', 0, 1), ('z', 7, 0), ('z', 1, 1), ('z', 2, 1), ('z', 3, 1), ('z', 4, 1), ('z', 5, 1), ('y', 0, 0, 4),
+    ('z', 6, 1), ('z', 0, 2), ('z', 7, 1), ('x', 2), ('z', 1, 2), ('z', 2, 2), ('z', 3, 2), ('z', 4, 2),
+    ('z', 5, 2), ('z', 6, 2), ('z', 0, 3), ('z', 7, 2), ('t', 0), ('y', 0, 1, 4), ('z', 1, 3), ('z', 2, 3),
+    ('z', 3, 3), ('z', 4, 3), ('z', 5, 3), ('z', 6, 3), ('f', 0), ('z', 7, 3), ('f', 1), ('f', 2),
+    ('f', 3), ('f', 4), ('f', 5), ('f', 6), ('f', 7), ('y', 1, 0, 4), ('t', 1), ('y', 0, 0, 3),
+    ('y', 1, 0, 3), ('y', 0, 1, 3), ('c', 11), ('z', 11, 0), ('x', 3), ('c', 13), ('y', 1, 1, 3), ('c', 18),
+    ('z', 11, 1), ('z', 13, 0), ('z', 18, 0), ('z', 11, 2), ('z', 13, 1), ('x', 4), ('peer',), ('z', 18, 1),
+    ('z', 11, 3), ('c', 16), ('z', 13, 2), ('c', 23), ('c', 26), ('z', 18, 2), ('z', 16, 0), ('c', 25),
+    ('z', 13, 3), ('z', 23, 0), ('c', 27), ('z', 26, 0), ('z', 18, 3), ('z', 16, 1), ('z', 25, 0), ('c', 21),
+    ('z', 23, 1), ('z', 26, 1), ('z', 27, 0), ('y', 1, 1, 4), ('f', 11), ('f', 13), ('f', 18), ('c', 14),
+    ('z', 16, 2), ('c', 15), ('z', 21, 0), ('z', 23, 2), ('z', 25, 1), ('z', 26, 2), ('z', 27, 1), ('z', 14, 0),
+    ('z', 16, 3), ('z', 15, 0), ('z', 21, 1), ('z', 23, 3), ('z', 25, 2), ('z', 26, 3), ('c', 10), ('z', 14, 1),
+    ('z', 27, 2), ('c', 12), ('z', 15, 1), ('c', 20), ('z', 21, 2), ('f', 16), ('f', 23), ('z', 25, 3),
+    ('z', 10, 0), ('c', 8), ('c', 24), ('z', 14, 2), ('z', 12, 0), ('f', 26), ('z', 27, 3), ('z', 20, 0),
+    ('z', 15, 2), ('z', 21, 3), ('c', 9), ('z', 8, 0), ('z', 10, 1), ('z', 24, 0), ('c', 17), ('z', 14, 3),
+    ('z', 12, 1), ('c', 19), ('c', 22), ('z', 20, 1), ('f', 25), ('f', 27), ('z', 15, 3), ('f', 21),
+    ('z', 9, 0), ('z', 8, 1), ('z', 17, 0), ('z', 10, 2), ('z', 24, 1), ('z', 19, 0), ('f', 14), ('z', 22, 0),
+    ('z', 12, 2), ('z', 20, 2), ('f', 15), ('z', 9, 1), ('m', 0, 0), ('z', 8, 2), ('z', 17, 1), ('z', 10, 3),
+    ('z', 24, 2), ('z', 19, 1), ('z', 22, 1), ('z', 12, 3), ('z', 20, 3), ('z', 9, 2), ('z', 8, 3), ('z', 17, 2),
+    ('f', 10), ('z', 24, 3), ('z', 19, 2), ('z', 22, 2), ('f', 12), ('f', 20), ('z', 9, 3), ('f', 8),
+    ('z', 17, 3), ('f', 24), ('z', 19, 3), ('z', 22, 3), ('u',), ('f', 9), ('f', 17), ('m', 0, 1),
+    ('m', 1, 0), ('f', 19), ('f', 22), ('m', 2, 0), ('m', 1, 1), ('own',), ('self',), ('next',),
+    ('m', 2, 1), ('far',),
 )
 
 
-def kernel(scale, a_ref, out_ref, G, Q, QP, RL, T, CR, ZR, R, PR, D, O1, O2, MB, MT, MO, OUT,
+def kernel(scale, a_ref, out_ref, G, Q, QP, RL, T, CR, ZR, R, PR, D, O1, O2, MB, MT, MO, DU, MTU, MOU, OUT,
            xs, xr, ys, yr, cs, cr, zs, zr, ds, dr, ms, mr, ts, tr, os):
     col, tok = lax.axis_index("col"), lax.axis_index("tok")
     lo, y = col // 4, col % 4
@@ -90,8 +103,8 @@
     sibling = at(x, y, z, 1 - c)
     z_dev = (at(x, y, (z + 1) % 8, c), at(x, y, (z + 7) % 8, c))
     far_lo = (lo + s) % 2
-    half_lo = {"p": lo, "r": lo, "0": 1 - lo, "1": 1 - lo, "f": far_lo, "g": far_lo}
-    half_h = {"p": hi, "r": 1 - hi, "0": 0, "1": 1, "f": hi, "g": 1 - hi}
+    half_lo = {"p": lo, "r": lo, "0": 1 - lo, "1": 1 - lo, "f": far_lo, "g": far_lo, "u": 1 - lo}
+    half_h = {"p": hi, "r": 1 - hi, "0": 0, "1": 1, "f": hi, "g": 1 - hi, "u": x_next // 2}
 
     def send(src, dst, s_sem, r_sem, dev):
         cp = pltpu.make_async_remote_copy(src_ref=src, dst_ref=dst, send_sem=s_sem, recv_sem=r_sem,
@@ -171,24 +184,16 @@
                 taken(y_landing(k, r, m), yr.at[2 * k + r, m])
 
     def x_step(n):
-        if n == 1:
-            need_x(0)
-            x_send(1, 4, 2, 5)
-        elif n == 2:
-            need_x(1)
-            turn(x_opposite, hi, A, Q.at[0, 1 - hi, A])
-            y_send(1, A, 0, 2, 1)
+        if n:
+            need_x(X_FORWARD[X_GROUPS[n][0]])
+        x_send(*X_GROUPS[n])
+
+    def q_step(r):
+        need_x((1, 3)[r])
+        turn(x_opposite, hi, r, Q.at[0, 1 - hi, r])
+        y_send(1, r, 0, 2, 1)
+        if r == A and not OWN_FIRST:
             y_send(0, B, 0, 2, 1)
-        elif n == 3:
-            need_x(2, 4)
-            x_send(3, 6, 7, 8, 9, 10)
-        elif n == 4:
-            need_x(3)
-            turn(x_opposite, hi, B, Q.at[0, 1 - hi, B])
-            y_send(1, B, 0, 2, 1)
-        else:
-            need_x(8)
-            x_send(11)
 
     def y_step(k, r, m):
         need_y(k, r, 0 if m == 3 else 2)
@@ -207,16 +212,21 @@
                 acc = jnp.dot(Q[kind - SELF, 0, r], G[l, h, cc], preferred_element_type=F32)
                 acc += jnp.dot(Q[kind - SELF, 1, r], G[2 + l, h, cc], preferred_element_type=F32)
             T[cell, :, :, :, j * CH:j * CH + CH] = acc.reshape(2, 8, PART, CH)
-        send(T.at[cell, 1 - c], CR.at[cell], cs.at[0], cr.at[cell], sibling)
-
-    sides = (pl.ds(0, CH), pl.ds(CH, CH))
+        w = width(cell)
+        send(T.at[cell, 1 - c, :, :, w], CR.at[cell, :, :, w], cs.at[0], cr.at[cell], sibling)
+
+    def width(cell):
+        return pl.ds(0, CH * len(CELLS[cell]))
 
     def z_landed(cell, step):
-        taken(ZR.at[cell, :, step] if step else ZR.at[cell, 0, 0], zr.at[cell, step])
+        w = width(cell)
+        taken(ZR.at[cell, :, step, :, w] if step else ZR.at[cell, 0, 0, :, w], zr.at[cell, step])
 
     def z_step(cell, step):
+        w, n = width(cell), CH * len(CELLS[cell]) // 2
+        sides = (pl.ds(0, n), pl.ds(n, n))
         if step == 0:
-            taken(CR.at[cell], cr.at[cell])
+            taken(CR.at[cell, :, :, w], cr.at[cell])
         else:
             z_landed(cell, step - 1)
         for d in range(2):
@@ -231,8 +241,8 @@
                 T[cell, c, to, :, cols] = T[cell, c, to, :, cols] + CR[cell, to, :, cols] + ZR[cell, d, 0, :, cols]
                 T[cell, c, to, :, rest] = T[cell, c, to, :, rest] + CR[cell, to, :, rest]
             else:
-                T[cell, c, to] = T[cell, c, to] + CR[cell, to] + ZR[cell, d, step - 1]
-            send(T.at[cell, c, to], ZR.at[cell, d, step], zs.at[0], zr.at[cell, step], z_dev[d])
+                T[cell, c, to, :, w] = T[cell, c, to, :, w] + CR[cell, to, :, w] + ZR[cell, d, step - 1, :, w]
+            send(T.at[cell, c, to, :, w], ZR.at[cell, d, step, :, w], zs.at[0], zr.at[cell, step], z_dev[d])
 
     def out_cols(l, y_):
         return pl.ds(pl.multiple_of((l * 4 + y_) * BLOCK, BLOCK), BLOCK)
@@ -245,16 +255,22 @@
 
     def finish(cell):
         z_landed(cell, 3)
-        R[cell] = T[cell, c, z] + CR[cell, z] + ZR[cell, 0, 3] + ZR[cell, 1, 3]
+        w = width(cell)
+        R[cell, :, w] = T[cell, c, z, :, w] + CR[cell, z, :, w] + ZR[cell, 0, 3, :, w] + ZR[cell, 1, 3, :, w]
         for j, (kind, r, half, cc) in enumerate(CELLS[cell]):
             l, h = half_lo[half], half_h[half]
             cols = pl.ds(j * CH, CH)
             src = R.at[cell, :, cols]
-            if kind in (OWN, SELF):
-                D[l, h, cc, r] = R[cell, :, cols]
+            if kind == OWN:
+                D[h, cc, r] = R[cell, :, cols]
+                continue
+            if kind == SELF:
+                DU[cc, r] = R[cell, :, cols]
+                for k in range(2):
+                    send(R.at[cell, :, pl.ds(j * CH + k * 128, 128)], MB.at[cc, 12 + c, r], ms.at[2], mr.at[3, 0],
+                         at(x_next, y, z, k))
                 continue
             if kind == PEER:
-                send(src, PR.at[h, cc, r], ds.at[0], dr.at[0], at(x_opposite, y, z, c))
                 continue
             if kind == NEXT:
                 send(src, O1.at[l, h, cc, r], ds.at[1], dr.at[1], y_up)
@@ -279,6 +295,12 @@
                 else:
                     pl.when(s == 0)(keep)
                     pl.when(s == 1)(leave)
+
+    def send_peer():
+        for cell, tiles in enumerate(CELLS):
+            for j, (kind, r, half, cc) in enumerate(tiles):
+                if kind == PEER:
+                    send(R.at[cell, :, pl.ds(j * CH, CH)], PR.at[half_h[half], cc, r], ds.at[0], dr.at[0], at(x_opposite, y, z, c))
 
     mirror_base = ((1 - lo) * 4, lo * 4, 8)
 
@@ -297,6 +319,15 @@
             to = (z + dz) % 8
             send(MT.at[b, cc, to], MO.at[b, z, cc], ts.at[0], tr.at[b, cc], at(x, y, to, c))
 
+    def mirror_next_x():
+        taken(MB.at[0, 0:4], mr.at[3, 0])
+        turned = [jnp.transpose(MB[cc, 12:14].reshape(2 * ROWS, 4 * ROWS)).reshape(8, PART, 2 * ROWS) for cc in (A, B)]
+        MTU[...] = jnp.concatenate(turned, axis=2) * scale
+        MOU[z] = MTU[z]
+        for dz in range(1, 8):
+            to = (z + dz) % 8
+            send(MTU.at[to], MOU.at[z], ts.at[1], tr.at[3, 0], at(x, y, to, c))
+
     def store(n, l, y_, v):
         OUT[n] = v
         pltpu.make_async_copy(OUT.at[n], out_ref.at[:, out_cols(l, y_)], os.at[0]).start()
@@ -313,7 +344,7 @@
 
     def store_own():
         taken(PR, dr.at[0])
-        store(0, lo, y, natural(D[lo] + PR[...]))
+        store(0, lo, y, natural(D[...] + PR[...]))
 
     def store_next():
         taken(O1, dr.at[1])
@@ -325,21 +356,32 @@
         store(3, (lo + 1 - s) % 2, y_far, natural(O2[...]))
 
     def store_self():
-        store(4, 1 - lo, y, natural(D[1 - lo]))
+        taken(MOU.at[0:7], tr.at[3, 0])
+        direct = [DU[cc].reshape(ROWS, CH) * scale for cc in (A, B)]
+        first = x_next // 2 == 0
+        groups = []
+        for b in range(8):
+            own = jnp.concatenate([direct[cc][:, k * 128 + b * PART:k * 128 + b * PART + PART]
+                                   for k in range(2) for cc in (A, B)], axis=1)
+            other = jnp.concatenate([MOU[b, :, cc * 64:cc * 64 + 64] for cc in (A, B)], axis=0)
+            groups += [jnp.where(first, own, other), jnp.where(first, other, own)]
+        store(4, 1 - lo, y, jnp.concatenate(groups, axis=1))
 
     for part in range(2):
         reorder(1 - hi, part)
     pl.semaphore_wait(barrier, len(partners))
-    x_send(0)
+    x_step(0)
     for part in range(2):
         reorder(hi, part)
     turn(x, hi, A, Q.at[0, hi, A])
     y_send(0, A, 0, 2, 1)
     turn(x, hi, B, Q.at[0, hi, B])
+    if OWN_FIRST:
+        y_send(0, B, 0, 2, 1)
     for cc in (A, B):
         turn(x, 1 - hi, cc, QP.at[cc])
 
-    steps = {"x": x_step, "y": y_step, "c": compute, "z": z_step, "f": finish, "m": mirror, "own": store_own, "next": store_next,
+    steps = {"x": x_step, "t": q_step, "u": mirror_next_x, "y": y_step, "c": compute, "z": z_step, "f": finish, "m": mirror, "peer": send_peer, "own": store_own, "next": store_next,
              "far": store_far, "self": store_self}
     for name, *given in ORDER:
         steps[name](*given)
@@ -350,14 +392,16 @@
     taken(G.at[0:3], xs.at[0])
     for m in range(5):
         taken(Q.at[0, :, :, low if m in (0, 3) else high], ys.at[m])
-    taken(CR, cs.at[0])
-    taken(CR.at[0:COUNT * 7 // 8], zs.at[0])
+    taken(CR.at[0:PAIRS], cs.at[0])
+    taken(CR.at[0:PAIRS, 0:7], zs.at[0])
     for n, ref in enumerate((PR, O1, O2)):
         taken(ref, ds.at[n])
     taken(MB.at[:, 0:7], ms.at[0])
     for v in range(2):
         pl.when(s == v)(lambda: taken(MB.at[:, 0:3 + v], ms.at[1]))
+    taken(MB.at[0, 0:4], ms.at[2])
     taken(MT.at[:, :, 0:7], ts.at[0])
+    taken(MTU.at[0:7], ts.at[1])
     taken(OUT, os.at[0])
 
 
@@ -382,20 +426,23 @@
                 pltpu.VMEM((COUNT, 2, 4, PART, HALF), F32),
                 pltpu.VMEM((COUNT, PART, HALF), F32),
                 pltpu.VMEM((2, 2, 2, PART, CH), F32),
-                pltpu.VMEM((2, 2, 2, 2, PART, CH), F32),
+                pltpu.VMEM((2, 2, 2, PART, CH), F32),
                 pltpu.VMEM((2, 2, 2, 2, PART, CH), F32),
                 pltpu.VMEM((2, 2, 2, PART, CH), F32),
-                pltpu.VMEM((2, 12, 2, PART, 4 * ROWS), F32),
+                pltpu.VMEM((2, 14, 2, PART, 4 * ROWS), F32),
                 pltpu.VMEM((3, 2, 8, PART, 4 * ROWS), F32),
                 pltpu.VMEM((3, 8, 2, PART, 4 * ROWS), F32),
+                pltpu.VMEM((2, 2, PART, CH), F32),
+                pltpu.VMEM((8, PART, 4 * ROWS), F32),
+                pltpu.VMEM((8, PART, 4 * ROWS), F32),
                 pltpu.VMEM((8, ROWS, BLOCK), F32),
                 dma((1,)), dma((12,)),
                 dma((5,)), dma((4, 5)),
                 dma((1,)), dma((COUNT,)),
                 dma((1,)), dma((COUNT, 4)),
                 dma((3,)), dma((3,)),
-                dma((2,)), dma((3, 2)),
-                dma((1,)), dma((3, 2)),
+                dma((3,)), dma((4, 2)),
+                dma((2,)), dma((4, 2)),
                 dma((1,)),
             ],
             compiler_params=pltpu.CompilerParams(

time: 127 us -> 120 us (0.945); the launches traced: 125 us -> 120 us
  Pallas kernels: 123 us -> 118 us
    pallas_call x1, Pallas kernels: 123 us -> 118 us  [shards(): pl.pallas_call(lambda *refs: kernel(scale, *refs), out_shape=jax.ShapeDty...]
where the time goes in v4:
time: 120 us
  Pallas kernels  118 us (98%)
  local copies, waits for them, and re-layouts  2.26 us (2%)
    pallas_call x1, Pallas kernels, shards(): pl.pallas_call(lambda *refs: kernel(scale, *refs), out_shape=jax.ShapeDty...  118 us

profile of v4, /device:TPU:1, one launch (start us, length us, event | category | flops | bytes accessed | tf_op | source)
XLA Modules:
  0.0 120.2 jit_solution(17448489320357136418)
XLA Ops:
  0.0 118.0 %gram.1 = f32[32,8192]{1,0:T(8,128)} custom-call(bf16[1024,1024]{1,0:T(8,128)(2,1)} %refs_0_.1), custom_call_target="tpu_custom_call" | custom-call | flops 14000000000 | bytes 3145728 | tf_op jit(solution)/shard_map/gram/pallas_call | solution.py:414
  118.0 2.3 %copy.3 = f32[32,8192]{1,0:T(8,128)} copy(f32[32,8192]{1,0:T(8,128)} %gram.1) | data formatting | bytes 2097152

commit v5 on v4

--- a/solution.py
+++ b/solution.py
@@ -25,26 +25,26 @@
     ((PEER, A, "r", A), (PEER, A, "r", B),),
     ((PEER, B, "p", A), (PEER, B, "p", B),),
     ((PEER, B, "r", A), (PEER, B, "r", B),),
-    ((FAR, B, "g", A),),
-    ((NEXT, A, "r", B), (FAR, B, "f", B),),
-    ((SELF, B, "u", B), (NEXT, B, "r", A),),
+    ((NEXT, A, "0", A), (SELF, B, "u", A),),
+    ((NEXT, A, "r", B), (NEXT, B, "r", B),),
+    ((FAR, A, "f", B), (NEXT, B, "0", B),),
+    ((FAR, A, "g", B), (FAR, B, "g", B),),
+    ((SELF, A, "u", B),),
+    ((NEXT, A, "1", A),),
     ((NEXT, A, "p", A),),
-    ((NEXT, A, "1", B), (NEXT, A, "r", A),),
-    ((SELF, B, "u", A),),
+    ((FAR, B, "f", B),),
+    ((NEXT, B, "p", A),),
+    ((NEXT, A, "p", B),),
+    ((NEXT, B, "r", A), (FAR, B, "g", A),),
+    ((NEXT, B, "p", B), (SELF, A, "u", A),),
+    ((NEXT, B, "0", A), (SELF, B, "u", B),),
+    ((FAR, B, "f", A),),
     ((NEXT, B, "1", B),),
-    ((SELF, A, "u", B), (FAR, A, "f", B),),
-    ((NEXT, B, "p", B), (NEXT, B, "1", A),),
-    ((NEXT, B, "r", B),),
-    ((NEXT, A, "1", A), (NEXT, A, "p", B),),
-    ((FAR, A, "g", B),),
     ((FAR, A, "g", A),),
+    ((NEXT, A, "0", B),),
+    ((NEXT, A, "1", B), (NEXT, B, "1", A),),
     ((FAR, A, "f", A),),
-    ((FAR, B, "g", B),),
-    ((NEXT, B, "p", A),),
-    ((FAR, B, "f", A),),
-    ((SELF, A, "u", A), (NEXT, A, "0", B),),
-    ((NEXT, A, "0", A), (NEXT, B, "0", A),),
-    ((NEXT, B, "0", B),),
+    ((NEXT, A, "r", A),),
 )
 COUNT = len(CELLS)
 PAIRS = sum(len(tiles) for tiles in CELLS) // 2
@@ -52,7 +52,7 @@
            ("1", A): (0, 4, 6), ("1", B): (2, 8, 10), ("f", A): (1, 0, 4, 5, 6), ("f", B): (3, 2, 8, 9, 10),
            ("g", A): (7, 0, 4, 5, 6), ("g", B): (11, 2, 8, 9, 10), ("u", A): (0, 4, 5, 6), ("u", B): (2, 8, 9, 10)}
 X_FORWARD = {1: 0, 3: 2, 7: 4, 11: 8}
-X_GROUPS = ((0, 2), (1, 6, 5), (3, 4, 8, 9, 10), (7,), (11,))
+X_GROUPS = ((0, 2), (1, 8, 5), (3, 4, 6, 10, 9), (11,), (7,))
 OWN_FIRST = True
 
 ORDER = (
@@ -61,30 +61,30 @@
     ('z', 0, 1), ('z', 7, 0), ('z', 1, 1), ('z', 2, 1), ('z', 3, 1), ('z', 4, 1), ('z', 5, 1), ('y', 0, 0, 4),
     ('z', 6, 1), ('z', 0, 2), ('z', 7, 1), ('x', 2), ('z', 1, 2), ('z', 2, 2), ('z', 3, 2), ('z', 4, 2),
     ('z', 5, 2), ('z', 6, 2), ('z', 0, 3), ('z', 7, 2), ('t', 0), ('y', 0, 1, 4), ('z', 1, 3), ('z', 2, 3),
-    ('z', 3, 3), ('z', 4, 3), ('z', 5, 3), ('z', 6, 3), ('f', 0), ('z', 7, 3), ('f', 1), ('f', 2),
-    ('f', 3), ('f', 4), ('f', 5), ('f', 6), ('f', 7), ('y', 1, 0, 4), ('t', 1), ('y', 0, 0, 3),
-    ('y', 1, 0, 3), ('y', 0, 1, 3), ('c', 11), ('z', 11, 0), ('x', 3), ('c', 13), ('y', 1, 1, 3), ('c', 18),
-    ('z', 11, 1), ('z', 13, 0), ('z', 18, 0), ('z', 11, 2), ('z', 13, 1), ('x', 4), ('peer',), ('z', 18, 1),
-    ('z', 11, 3), ('c', 16), ('z', 13, 2), ('c', 23), ('c', 26), ('z', 18, 2), ('z', 16, 0), ('c', 25),
-    ('z', 13, 3), ('z', 23, 0), ('c', 27), ('z', 26, 0), ('z', 18, 3), ('z', 16, 1), ('z', 25, 0), ('c', 21),
-    ('z', 23, 1), ('z', 26, 1), ('z', 27, 0), ('y', 1, 1, 4), ('f', 11), ('f', 13), ('f', 18), ('c', 14),
-    ('z', 16, 2), ('c', 15), ('z', 21, 0), ('z', 23, 2), ('z', 25, 1), ('z', 26, 2), ('z', 27, 1), ('z', 14, 0),
-    ('z', 16, 3), ('z', 15, 0), ('z', 21, 1), ('z', 23, 3), ('z', 25, 2), ('z', 26, 3), ('c', 10), ('z', 14, 1),
-    ('z', 27, 2), ('c', 12), ('z', 15, 1), ('c', 20), ('z', 21, 2), ('f', 16), ('f', 23), ('z', 25, 3),
-    ('z', 10, 0), ('c', 8), ('c', 24), ('z', 14, 2), ('z', 12, 0), ('f', 26), ('z', 27, 3), ('z', 20, 0),
-    ('z', 15, 2), ('z', 21, 3), ('c', 9), ('z', 8, 0), ('z', 10, 1), ('z', 24, 0), ('c', 17), ('z', 14, 3),
-    ('z', 12, 1), ('c', 19), ('c', 22), ('z', 20, 1), ('f', 25), ('f', 27), ('z', 15, 3), ('f', 21),
-    ('z', 9, 0), ('z', 8, 1), ('z', 17, 0), ('z', 10, 2), ('z', 24, 1), ('z', 19, 0), ('f', 14), ('z', 22, 0),
-    ('z', 12, 2), ('z', 20, 2), ('f', 15), ('z', 9, 1), ('m', 0, 0), ('z', 8, 2), ('z', 17, 1), ('z', 10, 3),
-    ('z', 24, 2), ('z', 19, 1), ('z', 22, 1), ('z', 12, 3), ('z', 20, 3), ('z', 9, 2), ('z', 8, 3), ('z', 17, 2),
-    ('f', 10), ('z', 24, 3), ('z', 19, 2), ('z', 22, 2), ('f', 12), ('f', 20), ('z', 9, 3), ('f', 8),
-    ('z', 17, 3), ('f', 24), ('z', 19, 3), ('z', 22, 3), ('u',), ('f', 9), ('f', 17), ('m', 0, 1),
-    ('m', 1, 0), ('f', 19), ('f', 22), ('m', 2, 0), ('m', 1, 1), ('own',), ('self',), ('next',),
-    ('m', 2, 1), ('far',),
+    ('z', 3, 3), ('z', 4, 3), ('z', 5, 3), ('z', 6, 3), ('f', 0), ('z', 7, 3), ('x', 3), ('f', 1),
+    ('f', 2), ('f', 3), ('f', 4), ('f', 5), ('f', 6), ('f', 7), ('y', 1, 0, 4), ('t', 1),
+    ('y', 0, 0, 3), ('y', 1, 0, 3), ('y', 0, 1, 3), ('c', 14), ('c', 17), ('z', 14, 0), ('z', 17, 0), ('x', 4),
+    ('peer',), ('y', 1, 1, 3), ('z', 14, 1), ('z', 17, 1), ('z', 14, 2), ('z', 17, 2), ('c', 8), ('c', 13),
+    ('z', 14, 3), ('z', 17, 3), ('c', 16), ('c', 19), ('z', 8, 0), ('z', 13, 0), ('z', 16, 0), ('c', 22),
+    ('z', 19, 0), ('c', 25), ('z', 8, 1), ('z', 13, 1), ('z', 16, 1), ('z', 22, 0), ('z', 19, 1), ('z', 25, 0),
+    ('c', 26), ('z', 8, 2), ('z', 13, 2), ('y', 1, 1, 4), ('f', 14), ('f', 17), ('z', 16, 2), ('z', 22, 1),
+    ('c', 10), ('z', 19, 2), ('c', 12), ('z', 25, 1), ('z', 26, 0), ('c', 20), ('z', 8, 3), ('z', 13, 3),
+    ('c', 24), ('z', 16, 3), ('z', 22, 2), ('z', 10, 0), ('z', 12, 0), ('z', 19, 3), ('z', 25, 2), ('z', 20, 0),
+    ('z', 26, 1), ('z', 24, 0), ('f', 8), ('c', 9), ('f', 13), ('z', 22, 3), ('f', 16), ('z', 10, 1),
+    ('z', 12, 1), ('f', 19), ('z', 25, 3), ('z', 9, 0), ('z', 20, 1), ('c', 11), ('z', 24, 1), ('z', 26, 2),
+    ('c', 15), ('c', 21), ('z', 10, 2), ('z', 12, 2), ('f', 22), ('c', 18), ('z', 9, 1), ('c', 23),
+    ('z', 11, 0), ('c', 27), ('z', 15, 0), ('z', 20, 2), ('z', 21, 0), ('z', 24, 2), ('z', 26, 3), ('f', 25),
+    ('z', 10, 3), ('z', 12, 3), ('z', 18, 0), ('z', 23, 0), ('z', 9, 2), ('z', 27, 0), ('z', 11, 1), ('z', 15, 1),
+    ('z', 20, 3), ('z', 21, 1), ('z', 24, 3), ('f', 26), ('f', 10), ('own',), ('f', 12), ('z', 18, 1),
+    ('z', 23, 1), ('z', 9, 3), ('z', 27, 1), ('z', 11, 2), ('z', 15, 2), ('f', 20), ('z', 21, 2), ('f', 24),
+    ('z', 18, 2), ('z', 23, 2), ('f', 9), ('z', 27, 2), ('z', 11, 3), ('z', 15, 3), ('z', 21, 3), ('z', 18, 3),
+    ('z', 23, 3), ('z', 27, 3), ('u',), ('m', 0, 0), ('m', 0, 1), ('f', 11), ('f', 15), ('f', 21),
+    ('f', 18), ('m', 1, 1), ('f', 23), ('f', 27), ('self',), ('m', 2, 1), ('m', 2, 0), ('m', 1, 0),
+    ('far',), ('next',),
 )
 
 
-def kernel(scale, a_ref, out_ref, G, Q, QP, RL, T, CR, ZR, R, PR, D, O1, O2, MB, MT, MO, DU, MTU, MOU, OUT,
+def kernel(scale, given_ref, out_ref, a_ref, G, Q, QP, RL, T, CR, ZR, R, PR, D, O1, O2, MB, MT, MO, DU, MTU, MOU,
            xs, xr, ys, yr, cs, cr, zs, zr, ds, dr, ms, mr, ts, tr, os):
     col, tok = lax.axis_index("col"), lax.axis_index("tok")
     lo, y = col // 4, col % 4
@@ -121,6 +121,8 @@
     barrier = pltpu.get_barrier_semaphore()
     for dev in partners:
         pl.semaphore_signal(barrier, inc=1, device_id=dev, device_id_type=MESH)
+    given = pltpu.make_async_copy(given_ref, a_ref, os.at[0])
+    given.start()
 
     def reorder(h, part):
         p = lax.broadcasted_iota(jnp.int32, (BLOCK, HALF), 1)
@@ -328,9 +330,8 @@
             to = (z + dz) % 8
             send(MTU.at[to], MOU.at[z], ts.at[1], tr.at[3, 0], at(x, y, to, c))
 
-    def store(n, l, y_, v):
-        OUT[n] = v
-        pltpu.make_async_copy(OUT.at[n], out_ref.at[:, out_cols(l, y_)], os.at[0]).start()
+    def store(l, y_, v):
+        out_ref[:, out_cols(l, y_)] = v
 
     def natural(v):
         t = [[v[h, cc].reshape(ROWS, CH) for cc in (A, B)] for h in range(2)]
@@ -340,20 +341,20 @@
     def store_mirror(b, l, y_):
         for cc in (A, B):
             taken(MO.at[b, 0:7, cc], tr.at[b, cc])
-        store(5 + b, l, y_, jnp.concatenate([MO[b, k].reshape(ROWS, 4 * ROWS) for k in range(8)], axis=1))
+        store(l, y_, jnp.concatenate([MO[b, k].reshape(ROWS, 4 * ROWS) for k in range(8)], axis=1))
 
     def store_own():
         taken(PR, dr.at[0])
-        store(0, lo, y, natural(D[...] + PR[...]))
+        store(lo, y, natural(D[...] + PR[...]))
 
     def store_next():
         taken(O1, dr.at[1])
         for l in range(2):
-            store(1 + l, l, y_prev, natural(O1[l]))
+            store(l, y_prev, natural(O1[l]))
 
     def store_far():
         taken(O2, dr.at[2])
-        store(3, (lo + 1 - s) % 2, y_far, natural(O2[...]))
+        store((lo + 1 - s) % 2, y_far, natural(O2[...]))
 
     def store_self():
         taken(MOU.at[0:7], tr.at[3, 0])
@@ -365,8 +366,9 @@
                                    for k in range(2) for cc in (A, B)], axis=1)
             other = jnp.concatenate([MOU[b, :, cc * 64:cc * 64 + 64] for cc in (A, B)], axis=0)
             groups += [jnp.where(first, own, other), jnp.where(first, other, own)]
-        store(4, 1 - lo, y, jnp.concatenate(groups, axis=1))
-
+        store(1 - lo, y, jnp.concatenate(groups, axis=1))
+
+    given.wait()
     for part in range(2):
         reorder(1 - hi, part)
     pl.semaphore_wait(barrier, len(partners))
@@ -383,8 +385,8 @@
 
     steps = {"x": x_step, "t": q_step, "u": mirror_next_x, "y": y_step, "c": compute, "z": z_step, "f": finish, "m": mirror, "peer": send_peer, "own": store_own, "next": store_next,
              "far": store_far, "self": store_self}
-    for name, *given in ORDER:
-        steps[name](*given)
+    for name, *which in ORDER:
+        steps[name](*which)
     store_mirror(0, 1 - lo, y_next)
     store_mirror(1, lo, y_next)
     store_mirror(2, far_lo, y_far)
@@ -402,7 +404,6 @@
     taken(MB.at[0, 0:4], ms.at[2])
     taken(MT.at[:, :, 0:7], ts.at[0])
     taken(MTU.at[0:7], ts.at[1])
-    taken(OUT, os.at[0])
 
 
 def solution(mesh):
@@ -413,10 +414,11 @@
         dma = pltpu.SemaphoreType.DMA
         return pl.pallas_call(
             lambda *refs: kernel(scale, *refs),
-            out_shape=jax.ShapeDtypeStruct((ROWS, 8 * BLOCK), F32),
-            in_specs=[pl.BlockSpec(memory_space=pltpu.VMEM)],
-            out_specs=pl.BlockSpec(memory_space=pl.ANY),
+            out_shape=pltpu.VMEM((ROWS, 8 * BLOCK), F32),
+            in_specs=[pl.BlockSpec(memory_space=pl.ANY)],
+            out_specs=pl.BlockSpec(memory_space=pltpu.VMEM),
             scratch_shapes=[
+                pltpu.VMEM((BLOCK, BLOCK), BF16),
                 pltpu.VMEM((4, 2, 2, BLOCK, CH), BF16),
                 pltpu.VMEM((3, 2, 2, CH, BLOCK), BF16),
                 pltpu.VMEM((2, CH, BLOCK), BF16),
@@ -435,7 +437,6 @@
                 pltpu.VMEM((2, 2, PART, CH), F32),
                 pltpu.VMEM((8, PART, 4 * ROWS), F32),
                 pltpu.VMEM((8, PART, 4 * ROWS), F32),
-                pltpu.VMEM((8, ROWS, BLOCK), F32),
                 dma((1,)), dma((12,)),
                 dma((5,)), dma((4, 5)),
                 dma((1,)), dma((COUNT,)),

time: 120 us -> 117 us (0.975)
  Pallas kernels: 118 us -> 115 us
  local copies, waits for them, and re-layouts: 2.26 us -> 0.97 us
    pallas_call x1, Pallas kernels: 118 us -> 115 us  [shards(): pl.pallas_call(lambda *refs: kernel(scale, *refs), out_shape=pltpu.VMEM((...]
    unnamed x1, local copies, waits for them, and re-layouts: 2.26 us -> 0.97 us
where the time goes in v5:
time: 117 us; the launch traced here: 116 us
  Pallas kernels  115 us (98%)
    pallas_call x1, Pallas kernels, shards(): pl.pallas_call(lambda *refs: kernel(scale, *refs), out_shape=pltpu.VMEM((...  115 us

profile of v5, /device:TPU:1, one launch (start us, length us, event | category | flops | bytes accessed | tf_op | source)
XLA Modules:
  0.0 116.5 jit_solution(16681336754161226958)
XLA Ops:
  0.0 115.5 %gram.1 = f32[32,8192]{1,0:T(8,128)S(1)} custom-call(bf16[1024,1024]{1,0:T(8,128)(2,1)} %refs_0_.1), custom_call_target="tpu_custom_call" | custom-call | flops 14000000000 | bytes 3145728 | tf_op jit(solution)/shard_map/gram/pallas_call | solution.py:415
  115.5 1.0 copy.3

commit v6 on v5

--- a/solution.py
+++ b/solution.py
@@ -71,16 +71,16 @@
     ('c', 10), ('z', 19, 2), ('c', 12), ('z', 25, 1), ('z', 26, 0), ('c', 20), ('z', 8, 3), ('z', 13, 3),
     ('c', 24), ('z', 16, 3), ('z', 22, 2), ('z', 10, 0), ('z', 12, 0), ('z', 19, 3), ('z', 25, 2), ('z', 20, 0),
     ('z', 26, 1), ('z', 24, 0), ('f', 8), ('c', 9), ('f', 13), ('z', 22, 3), ('f', 16), ('z', 10, 1),
-    ('z', 12, 1), ('f', 19), ('z', 25, 3), ('z', 9, 0), ('z', 20, 1), ('c', 11), ('z', 24, 1), ('z', 26, 2),
-    ('c', 15), ('c', 21), ('z', 10, 2), ('z', 12, 2), ('f', 22), ('c', 18), ('z', 9, 1), ('c', 23),
-    ('z', 11, 0), ('c', 27), ('z', 15, 0), ('z', 20, 2), ('z', 21, 0), ('z', 24, 2), ('z', 26, 3), ('f', 25),
+    ('z', 12, 1), ('f', 19), ('z', 25, 3), ('z', 9, 0), ('z', 20, 1), ('z', 24, 1), ('z', 26, 2), ('c', 11),
+    ('c', 15), ('z', 10, 2), ('z', 12, 2), ('c', 21), ('z', 20, 2), ('z', 9, 1), ('c', 18), ('z', 24, 2),
+    ('z', 26, 3), ('z', 11, 0), ('c', 23), ('z', 15, 0), ('f', 22), ('c', 27), ('z', 21, 0), ('f', 25),
     ('z', 10, 3), ('z', 12, 3), ('z', 18, 0), ('z', 23, 0), ('z', 9, 2), ('z', 27, 0), ('z', 11, 1), ('z', 15, 1),
     ('z', 20, 3), ('z', 21, 1), ('z', 24, 3), ('f', 26), ('f', 10), ('own',), ('f', 12), ('z', 18, 1),
     ('z', 23, 1), ('z', 9, 3), ('z', 27, 1), ('z', 11, 2), ('z', 15, 2), ('f', 20), ('z', 21, 2), ('f', 24),
     ('z', 18, 2), ('z', 23, 2), ('f', 9), ('z', 27, 2), ('z', 11, 3), ('z', 15, 3), ('z', 21, 3), ('z', 18, 3),
     ('z', 23, 3), ('z', 27, 3), ('u',), ('m', 0, 0), ('m', 0, 1), ('f', 11), ('f', 15), ('f', 21),
-    ('f', 18), ('m', 1, 1), ('f', 23), ('f', 27), ('self',), ('m', 2, 1), ('m', 2, 0), ('m', 1, 0),
-    ('far',), ('next',),
+    ('f', 18), ('m', 1, 1), ('f', 23), ('f', 27), ('m', 2, 1), ('m', 2, 0), ('m', 1, 0), ('next',),
+    ('self',), ('far',),
 )
 
 
@@ -274,10 +274,6 @@
                 continue
             if kind == PEER:
                 continue
-            if kind == NEXT:
-                send(src, O1.at[l, h, cc, r], ds.at[1], dr.at[1], y_up)
-            else:
-                send(src, O2.at[h, cc, r], ds.at[2], dr.at[2], at(x, y_far, z, c))
             mine = (8 if kind == FAR else lo * 4) + hi * 2 + c
             s_sem, batch = ms.at[kind - NEXT], 2 if kind == FAR else 1 if half in "pr" else 0
             for dk in range(2):
@@ -297,6 +293,10 @@
                 else:
                     pl.when(s == 0)(keep)
                     pl.when(s == 1)(leave)
+            if kind == NEXT:
+                send(src, O1.at[l, h, cc, r], ds.at[1], dr.at[1], y_up)
+            else:
+                send(src, O2.at[h, cc, r], ds.at[2], dr.at[2], at(x, y_far, z, c))
 
     def send_peer():
         for cell, tiles in enumerate(CELLS):

time: 117 us -> 116 us (level)
    pallas_call x1, Pallas kernels: 115 us -> 114 us  [shards(): pl.pallas_call(lambda *refs: kernel(scale, *refs), out_shape=pltpu.VMEM((...]
where the time goes in v6:
time: 116 us; the launch traced here: 115 us
  Pallas kernels  114 us (98%)
    pallas_call x1, Pallas kernels, shards(): pl.pallas_call(lambda *refs: kernel(scale, *refs), out_shape=pltpu.VMEM((...  114 us

profile of v6, /device:TPU:1, one launch (start us, length us, event | category | flops | bytes accessed | tf_op | source)
XLA Modules:
  0.0 115.1 jit_solution(15487784386393442723)
XLA Ops:
  0.0 114.1 %gram.1 = f32[32,8192]{1,0:T(8,128)S(1)} custom-call(bf16[1024,1024]{1,0:T(8,128)(2,1)} %refs_0_.1), custom_call_target="tpu_custom_call" | custom-call | flops 14000000000 | bytes 3145728 | tf_op jit(solution)/shard_map/gram/pallas_call | solution.py:415
  114.1 1.0 copy.3

commit v7 on v6

--- a/solution.py
+++ b/solution.py
@@ -52,7 +52,7 @@
            ("1", A): (0, 4, 6), ("1", B): (2, 8, 10), ("f", A): (1, 0, 4, 5, 6), ("f", B): (3, 2, 8, 9, 10),
            ("g", A): (7, 0, 4, 5, 6), ("g", B): (11, 2, 8, 9, 10), ("u", A): (0, 4, 5, 6), ("u", B): (2, 8, 9, 10)}
 X_FORWARD = {1: 0, 3: 2, 7: 4, 11: 8}
-X_GROUPS = ((0, 2), (1, 8, 5), (3, 4, 6, 10, 9), (11,), (7,))
+X_GROUPS = ((0, 2), (1, 5), (3, 4, 6, 8, 10, 9), (11,), (7,))
 OWN_FIRST = True
 
 ORDER = (
@@ -61,14 +61,14 @@
     ('z', 0, 1), ('z', 7, 0), ('z', 1, 1), ('z', 2, 1), ('z', 3, 1), ('z', 4, 1), ('z', 5, 1), ('y', 0, 0, 4),
     ('z', 6, 1), ('z', 0, 2), ('z', 7, 1), ('x', 2), ('z', 1, 2), ('z', 2, 2), ('z', 3, 2), ('z', 4, 2),
     ('z', 5, 2), ('z', 6, 2), ('z', 0, 3), ('z', 7, 2), ('t', 0), ('y', 0, 1, 4), ('z', 1, 3), ('z', 2, 3),
-    ('z', 3, 3), ('z', 4, 3), ('z', 5, 3), ('z', 6, 3), ('f', 0), ('z', 7, 3), ('x', 3), ('f', 1),
-    ('f', 2), ('f', 3), ('f', 4), ('f', 5), ('f', 6), ('f', 7), ('y', 1, 0, 4), ('t', 1),
-    ('y', 0, 0, 3), ('y', 1, 0, 3), ('y', 0, 1, 3), ('c', 14), ('c', 17), ('z', 14, 0), ('z', 17, 0), ('x', 4),
-    ('peer',), ('y', 1, 1, 3), ('z', 14, 1), ('z', 17, 1), ('z', 14, 2), ('z', 17, 2), ('c', 8), ('c', 13),
-    ('z', 14, 3), ('z', 17, 3), ('c', 16), ('c', 19), ('z', 8, 0), ('z', 13, 0), ('z', 16, 0), ('c', 22),
-    ('z', 19, 0), ('c', 25), ('z', 8, 1), ('z', 13, 1), ('z', 16, 1), ('z', 22, 0), ('z', 19, 1), ('z', 25, 0),
-    ('c', 26), ('z', 8, 2), ('z', 13, 2), ('y', 1, 1, 4), ('f', 14), ('f', 17), ('z', 16, 2), ('z', 22, 1),
-    ('c', 10), ('z', 19, 2), ('c', 12), ('z', 25, 1), ('z', 26, 0), ('c', 20), ('z', 8, 3), ('z', 13, 3),
+    ('z', 3, 3), ('z', 4, 3), ('z', 5, 3), ('z', 6, 3), ('f', 0), ('z', 7, 3), ('f', 1), ('f', 2),
+    ('f', 3), ('f', 4), ('f', 5), ('f', 6), ('f', 7), ('t', 1), ('y', 1, 0, 4), ('y', 0, 0, 3),
+    ('y', 1, 0, 3), ('y', 0, 1, 3), ('c', 14), ('c', 17), ('z', 14, 0), ('z', 17, 0), ('c', 8), ('c', 13),
+    ('z', 14, 1), ('z', 17, 1), ('z', 8, 0), ('z', 13, 0), ('z', 14, 2), ('z', 17, 2), ('y', 1, 1, 3), ('z', 8, 1),
+    ('z', 13, 1), ('z', 14, 3), ('z', 17, 3), ('c', 16), ('c', 19), ('x', 3), ('x', 4), ('peer',),
+    ('z', 8, 2), ('z', 13, 2), ('z', 16, 0), ('c', 22), ('z', 19, 0), ('c', 25), ('z', 8, 3), ('z', 13, 3),
+    ('z', 16, 1), ('z', 22, 0), ('z', 19, 1), ('z', 25, 0), ('c', 26), ('y', 1, 1, 4), ('f', 14), ('f', 17),
+    ('z', 16, 2), ('z', 22, 1), ('c', 10), ('z', 19, 2), ('c', 12), ('z', 25, 1), ('z', 26, 0), ('c', 20),
     ('c', 24), ('z', 16, 3), ('z', 22, 2), ('z', 10, 0), ('z', 12, 0), ('z', 19, 3), ('z', 25, 2), ('z', 20, 0),
     ('z', 26, 1), ('z', 24, 0), ('f', 8), ('c', 9), ('f', 13), ('z', 22, 3), ('f', 16), ('z', 10, 1),
     ('z', 12, 1), ('f', 19), ('z', 25, 3), ('z', 9, 0), ('z', 20, 1), ('z', 24, 1), ('z', 26, 2), ('c', 11),

time: 116 us -> 116 us (level)
  no operation moved by 1% of the time
where the time goes in v7:
time: 116 us
  Pallas kernels  115 us (99%)
    pallas_call x1, Pallas kernels, shards(): pl.pallas_call(lambda *refs: kernel(scale, *refs), out_shape=pltpu.VMEM((...  115 us

profile of v7, /device:TPU:1, one launch (start us, length us, event | category | flops | bytes accessed | tf_op | source)
XLA Modules:
  0.0 115.6 jit_solution(1508962635336089279)
XLA Ops:
  0.0 114.6 %gram.1 = f32[32,8192]{1,0:T(8,128)S(1)} custom-call(bf16[1024,1024]{1,0:T(8,128)(2,1)} %refs_0_.1), custom_call_target="tpu_custom_call" | custom-call | flops 14000000000 | bytes 3145728 | tf_op jit(solution)/shard_map/gram/pallas_call | solution.py:415
  114.6 1.0 copy.3
